TPU v7x, 256 devices: a whole 4x4x8 slice. The times are simulated.
256 devices in a mesh: view: 4 (over z_hi), block: 64 (over y, x, z_lo, core).
Axes of the slice: x: 4, y: 4, z: 8 (z_hi: 4, z_lo: 2; z = z_hi * 2 + z_lo), core: 2. Of those that a mesh axis runs over, the one named last changes fastest.
Arguments:
- view_tiles: bfloat16 [4, 5120, 24, 1024], P('view', 'block'), may hold values from 0.25 to 4
- route_block: int32 [4, 5120], P('view', 'block'), may hold values from 0 to 63, as said below
- route_column: int32 [4, 5120], P('view', 'block'), may hold values from 0 to 31, as said below
- psf_taps: float32 [4, 3, 31], P('view'), may hold values from 0.002 to 1.5
- start_estimate: float32 [24, 2048, 1024], P(None, 'block'), may hold values from 0.5 to 2
Outputs:
- estimate: float32 [24, 2048, 1024], P(None, 'block')
Inputs may be any that keep to these rules, and one draw needn't show every extreme that they name: `route_block`: for each view, every column of every block receives at least one tile column; at most 2 tile columns held by one device go to one block, and in every draw some block receives exactly 2 from every device. `route_column`: column within the receiving block.
All inputs are finite; a program needn't handle non-finite values.
Results may differ from a plain program's by a relative error of at most 0.00071.
Values may be sent and summed in bfloat16 or wider, within the bound.
No kernel may reach another device: no remote copies, remote signals or barrier semaphores. Data moves between devices by JAX's collectives and lax.ppermute only.
A program may use at most 128 MiB of HBM per device.

v0:
```python
import functools

import jax
import jax.numpy as jnp
import numpy as np
from jax import lax
from jax.experimental import pallas as pl
from jax.experimental.pallas import tpu as pltpu
from jax.sharding import PartitionSpec as P

ITERS = 2
TAPS = 31
HALF = 15
VIEWS = 4
NZ = 24
BX = 32
MARGIN = 16
EX = BX + 2 * MARGIN
YQ = 256
YE = 384
TURN = 320
ROWS = BX * NZ
ZI = 8
ZG = NZ // ZI
XR = BX * ZI
EXR = EX * ZI
GX = 8
GR = GX * ZI
ZR = GX * NZ
FULL = 32700.0
STEPS = 128.0
LN2 = float(np.log(2.0))
M_MID, M_SCALE = 2.125, 32767.0 / 1.875
E_SCALE = 32767.0 / 2.0
VMEM = 28 * 1024 * 1024

f32, bf16, i32, i16 = jnp.float32, jnp.bfloat16, jnp.int32, jnp.int16


def params(limit=VMEM):
    return pltpu.CompilerParams(vmem_limit_bytes=limit)


KEPT = pl.BlockSpec(memory_space=pltpu.VMEM)


def kept(operands):
    return [pltpu.with_memory_space_constraint(x, pltpu.VMEM) for x in operands]


def cost(flops, moved):
    return pl.CostEstimate(flops=int(flops), bytes_accessed=int(moved), transcendentals=0)


def dot(a, b):
    return jnp.dot(a, b, preferred_element_type=f32)


def to_code(x):
    return jnp.floor(x + 0.5).astype(i32).astype(i16)


def from_code(c):
    return c.astype(i32).astype(f32)


def scale_steps(top):
    return jnp.ceil(jnp.log(jnp.maximum(top, 1e-30)) * (STEPS / LN2))


def lane_code(value):
    k = scale_steps(jnp.max(jnp.abs(value), axis=0, keepdims=True))
    code = to_code(value * (jnp.exp(k * (-LN2 / STEPS)) * FULL))
    return code, jnp.broadcast_to(k, (16, value.shape[1])).astype(i32).astype(i16)


def lane_value(ref):
    n = ref.shape[0] - 16
    k = from_code(ref[n:])[0:1]
    return from_code(ref[:n]) * (jnp.exp(k * (LN2 / STEPS)) * (1.0 / FULL))


def send(ref, value):
    n = value.shape[0]
    ref[:n], ref[n:] = lane_code(value)


def margin_lanes(shape):
    lane = lax.broadcasted_iota(i32, shape, 1)
    return (lane < 32) | (lane >= 96)


def send_wide(ref, value):
    n = value.shape[0]
    k = scale_steps(jnp.max(jnp.abs(value), axis=0, keepdims=True))
    scaled = value * (jnp.exp(k * (-LN2 / STEPS)) * FULL)
    ref[:n] = to_code(scaled[:, :YQ])
    first, second = scaled[: n // 2, YQ:], scaled[n // 2 :, YQ:]
    shared = jnp.where(margin_lanes(first.shape), first, pltpu.roll(second, 64, 1))
    shared = jnp.concatenate([shared[: n // 4], shared[n // 4 :]], axis=1)
    ref[n : n + n // 4] = to_code(shared)
    k = jnp.concatenate([k[:, :YQ], k[:, YQ:], k[:, YQ:]], axis=1)
    k = jnp.broadcast_to(k, (16, 2 * YQ)).astype(i32).astype(i16)
    ref[n + n // 4 : n + n // 4 + 16] = k[:, :YQ]
    ref[n + n // 4 + 16 :] = k[:, YQ:]


def wide_rows(n):
    return n + n // 4 + 32


def wide_value(ref):
    n = (ref.shape[0] - 32) * 4 // 5
    at = n + n // 4
    center = from_code(ref[:n]) * (jnp.exp(from_code(ref[at : at + 16])[0:1] * (LN2 / STEPS)) / FULL)
    shared = from_code(ref[n:at])
    shared = jnp.concatenate([shared[:, :128], shared[:, 128:]], axis=0)
    ours = margin_lanes(shared.shape)
    first = jnp.where(ours, shared, 0.0)
    second = pltpu.roll(jnp.where(ours, 0.0, shared), 64, 1)
    k = from_code(ref[at + 16 :])[0:1, :128]
    ends = jnp.concatenate([first, second], axis=0) * (jnp.exp(k * (LN2 / STEPS)) / FULL)
    return jnp.concatenate([center, ends], axis=1)


def flat(x):
    return x.reshape(x.shape[0] * x.shape[1], x.shape[2])


def send_sides(encode, place, first, second, left, right, sides):
    encode(sides.at[0], left)
    encode(sides.at[1], right)
    even = lax.rem(place[0], 2) == 0

    @pl.when(even)
    def _():
        first[...], second[...] = sides[0], sides[1]

    @pl.when(jnp.logical_not(even))
    def _():
        first[...], second[...] = sides[1], sides[0]


def take_sides(place, first, second, sides):
    even = lax.rem(place[0], 2) == 0

    @pl.when(even)
    def _():
        sides[0], sides[1] = first[...], second[...]

    @pl.when(jnp.logical_not(even))
    def _():
        sides[0], sides[1] = second[...], first[...]


LOADS = 4
SLOT = NZ * 8


def pack_body(cap, blocks, columns, tiles, out, labels, count, slots, held, sent, loaded, pushed):
    pieces = tiles.shape[0]
    part = pieces // LOADS
    groups = out.shape[0]

    def load(i):
        rows = pl.ds(i * part, part)
        return pltpu.make_async_copy(tiles.at[rows], held.at[rows], loaded.at[i])

    for i in range(LOADS):
        load(i).start()

    def clear(i, _):
        labels[i] = 0
        return 0

    lax.fori_loop(0, groups * cap, clear, 0)

    def zero(i, _):
        count[i] = 0
        return 0

    lax.fori_loop(0, groups, zero, 0)

    def route(p, _):
        b = blocks[p]
        rank = count[b]
        count[b] = rank + 1
        slot = b * cap + rank
        labels[slot] = columns[p] + 1
        slots[p] = slot
        return 0

    lax.fori_loop(0, pieces, route, 0)
    lane = lax.broadcasted_iota(i32, (16, 128), 1)

    def mark(b, _):
        row = jnp.zeros((16, 128), i32)
        for rank in range(cap):
            row = jnp.where(lane == rank, labels[b * cap + rank], row)
        sent[b, cap * SLOT :, :] = row.astype(f32).astype(bf16)
        return 0

    lax.fori_loop(0, groups, mark, 0)
    def push(b, at, rows, sem):
        part = pl.ds(pl.multiple_of(at, 16), rows)
        return pltpu.make_async_copy(sent.at[b, part, :], out.at[b, part, :], sem)

    def tags():
        rows = pl.ds(cap * SLOT, 16)
        return pltpu.make_async_copy(sent.at[:, rows, :], out.at[:, rows, :], pushed.at[1])

    tags().start()
    for i in range(LOADS):
        load(i).wait()

        def put(p, _):
            slot = slots[p]
            b = slot // cap
            at = (slot - b * cap) * SLOT
            for c in range(8):
                rows = pl.ds(pl.multiple_of(at + 16 * c, 16), 16)
                sent[b, rows, :] = held[p, :16, 128 * c : 128 * (c + 1)]
            for c in range(0, 8, 2):
                rows = pl.ds(pl.multiple_of(at + 128 + 8 * c, 16), 16)
                sent[b, rows, :] = jnp.concatenate(
                    [
                        held[p, 16:, 128 * c : 128 * (c + 1)],
                        held[p, 16:, 128 * (c + 1) : 128 * (c + 2)],
                    ],
                    axis=0,
                )
            push(b, at, SLOT, pushed.at[0]).start()
            return 0

        lax.fori_loop(i * part, (i + 1) * part, put, 0, unroll=2)
    tags().wait()
    if pieces % cap == 0:
        every = pl.ds(0, pieces // cap), pl.ds(0, cap * SLOT)
        pltpu.make_async_copy(sent.at[every], out.at[every], pushed.at[0]).wait()
    else:
        lax.fori_loop(0, pieces, lambda p, _: push(0, 0, SLOT, pushed.at[0]).wait(), None)


def pack(cap, groups, blocks, columns, tiles):
    smem = pl.BlockSpec(memory_space=pltpu.SMEM)
    message = (groups, cap * SLOT + 16, 128)
    return pl.pallas_call(
        functools.partial(pack_body, cap),
        out_shape=pltpu.HBM(message, bf16),
        in_specs=[smem, smem, pl.BlockSpec(memory_space=pltpu.HBM)],
        out_specs=pl.BlockSpec(memory_space=pltpu.HBM),
        scratch_shapes=[
            pltpu.SMEM((groups * cap,), i32),
            pltpu.SMEM((groups,), i32),
            pltpu.SMEM((tiles.shape[0],), i32),
            pltpu.VMEM(tiles.shape, bf16),
            pltpu.VMEM(message, bf16),
            pltpu.SemaphoreType.DMA((LOADS,)),
            pltpu.SemaphoreType.DMA((2,)),
        ],
        compiler_params=params(2 * VMEM),
        cost_estimate=cost(0, 4 * tiles.size),
    )(blocks, columns, pltpu.with_memory_space_constraint(tiles, pltpu.HBM))


PART_VIEWS = (0, 1, 2, 2, 3)
PART_ROWS = (0, 0, 0, ROWS // 2, 0)


def unpack_body(cap, chunk, place, arrived, whole_arrived, *rest):
    outs, (acc, codes, count, marks, table, labels, sem) = rest[: VIEWS + 1], rest[VIEWS + 1 :]
    step = pl.program_id(0)
    layer = place[1]

    @pl.when(step == 0)
    def _():
        fetch = pltpu.make_async_copy(
            whole_arrived.at[:, pl.ds(cap * SLOT, 16), :], marks, sem.at[0]
        )
        fetch.start()
        acc[...] = jnp.zeros_like(acc)

        def zero(i, _):
            count[i] = 0
            return 0

        lax.fori_loop(0, BX, zero, 0)
        fetch.wait()
        ranks = table.shape[0]
        which = jnp.where(iota((ranks, 128), 0) == iota((ranks, 128), 1), 1.0, 0.0)
        lines = jnp.max(marks[...].astype(f32), axis=1)
        found = lax.dot_general(which, lines, (((1,), (1,)), ((), ())), preferred_element_type=f32)
        table[:, : lines.shape[0]] = found.astype(i32)
        move = pltpu.make_async_copy(table, labels, sem.at[1])
        move.start()
        move.wait()

    def from_source(j, _):
        for rank in range(cap):
            label = labels[rank, step * chunk + j]

            @pl.when(label > 0)
            def _():
                col = label - 1
                rows = pl.ds(pl.multiple_of(col * ZI, ZI), ZI)
                tile = arrived[j, rank * SLOT : (rank + 1) * SLOT, :].astype(f32)
                for c in range(8):
                    lanes = slice(128 * c, 128 * (c + 1))
                    acc[0, rows, lanes] += tile[16 * c : 16 * c + 8]
                    acc[1, rows, lanes] += tile[16 * c + 8 : 16 * c + 16]
                    acc[2, rows, lanes] += tile[128 + 8 * c : 136 + 8 * c]
                count[col] += 1

        return 0

    lax.fori_loop(0, chunk, from_source, 0, unroll=4)

    @pl.when(step == pl.num_programs(0) - 1)
    def _():
        row = lax.broadcasted_iota(i32, (2 * ZI, 128), 0)
        lane = lax.broadcasted_iota(i32, (2 * ZI, 128), 1)

        def pair(i, _):
            first = M_SCALE / jnp.maximum(count[2 * i], 1).astype(f32)
            second = M_SCALE / jnp.maximum(count[2 * i + 1], 1).astype(f32)
            inverse = jnp.where(row < ZI, first, second)
            for g in range(ZG):
                rows = pl.ds(pl.multiple_of(i * 2 * ZI, 2 * ZI), 2 * ZI)
                to = pl.ds(pl.multiple_of(g * XR + i * 2 * ZI, 2 * ZI), 2 * ZI)
                blocks = [
                    acc[g, rows, 128 * c : 128 * (c + 1)] * inverse - M_MID * M_SCALE
                    for c in range(2 * VIEWS)
                ]
                for v in range(VIEWS):
                    after = blocks[min(2 * v + 2, 2 * VIEWS - 1)]
                    before = blocks[max(2 * v - 1, 0)]
                    ends = jnp.where(lane < 64, after, before)
                    code = jnp.concatenate([blocks[2 * v], blocks[2 * v + 1], ends], axis=1)
                    codes[v, to, :] = to_code(code)
            return 0

        lax.fori_loop(0, BX // 2, pair, 0, unroll=2)
        for r, at, out in zip(PART_VIEWS, PART_ROWS, outs):
            out[...] = codes[lax.rem(layer + r, VIEWS), at : at + out.shape[0], :]


def unpack(cap, place, arrived):
    groups = arrived.shape[0]
    chunk = min(32, groups)
    shapes = [(ROWS // PART_VIEWS.count(r), YE) for r in PART_VIEWS]
    smem = pl.BlockSpec(memory_space=pltpu.SMEM)
    return pl.pallas_call(
        functools.partial(unpack_body, cap, chunk),
        grid=(groups // chunk,),
        out_shape=tuple(jax.ShapeDtypeStruct(shape, i16) for shape in shapes),
        in_specs=[
            smem,
            pl.BlockSpec((chunk,) + arrived.shape[1:], lambda s: (s, 0, 0)),
            pl.BlockSpec(memory_space=pl.ANY),
        ],
        out_specs=tuple(pl.BlockSpec(shape, lambda s: (0, 0)) for shape in shapes),
        scratch_shapes=[
            pltpu.VMEM((ZG, XR, VIEWS * YQ), f32),
            pltpu.VMEM((VIEWS, ROWS, YE), i16),
            pltpu.SMEM((BX,), i32),
            pltpu.VMEM((groups, 16, 128), bf16),
            pltpu.VMEM((max(8, cap), 128), i32),
            pltpu.SMEM((max(8, cap), 128), i32),
            pltpu.SemaphoreType.DMA((2,)),
        ],
        compiler_params=params(),
        cost_estimate=cost(arrived.size, 2 * arrived.size),
    )(place, arrived, arrived)


def iota(shape, dim):
    return lax.broadcasted_iota(i32, shape, dim)


def bands_body(taps, kx, kxt, ty, tyt, bz, bzt):
    r = pl.program_id(0)

    def band(distance, axis):
        out = jnp.zeros(distance.shape, f32)
        for t in range(TAPS):
            out = jnp.where(distance == t, taps[r, axis * TAPS + t], out)
        return out

    def circulant(row, n):
        wide = jnp.broadcast_to(row[0:1], (n, row.shape[1]))
        return pltpu.roll(wide, 0, 1, stride=1, stride_axis=0).astype(bf16)

    m = iota((8, EXR), 1)
    aligned = lax.bitwise_and(m, ZI - 1) == 0
    taps_at = band(lax.shift_right_logical(m, 3) - 1, 1)
    kx[r] = circulant(jnp.where(aligned, taps_at, 0.0), XR)
    taps_at = band(lax.shift_right_logical(EXR - m, 3) - 1, 1)
    kxt[r] = circulant(jnp.where(aligned, taps_at, 0.0), EXR)[:, :XR]
    n = iota((8, YE), 1)
    apart = jnp.where(n < YE // 2, n, n - YE)
    ty[r] = circulant(band(HALF - apart, 2), YE)
    back = circulant(band(HALF + apart, 2), YE)
    tyt[r] = back

    def parts(x):
        group = jnp.where(x >= 2 * GR, 2, jnp.where(x >= GR, 1, 0))
        within = x - group * GR
        return group * ZI + lax.bitwise_and(within, ZI - 1), lax.shift_right_logical(within, 3)

    (zr, xr), (zc, xc) = parts(iota((ZR, 1), 0)), parts(iota((1, ZR), 1))
    same = xr == xc
    bz[r] = jnp.where(same, band(zc - zr + HALF, 0), 0.0).astype(bf16)
    bzt[r] = jnp.where(same, band(zr - zc + HALF, 0), 0.0).astype(bf16)


MATS = [(XR, EXR), (EXR, XR), (YE, YE), (YE, YE), (ZR, ZR), (ZR, ZR)]


def bands(taps):
    return pl.pallas_call(
        bands_body,
        grid=(VIEWS,),
        out_shape=tuple(pltpu.VMEM((VIEWS,) + s, bf16) for s in MATS),
        in_specs=[pl.BlockSpec(memory_space=pltpu.SMEM)],
        out_specs=(KEPT,) * len(MATS),
        compiler_params=params(),
        cost_estimate=cost(4e9, 2e7),
    )(taps)


def cell_body(place, start, own, left, right, scratch):
    layer = place[1]
    last = start.shape[2] - 128
    after = jnp.minimum((layer + 1) * YQ, last)
    before = jnp.maximum(layer * YQ - 128, 0)
    lane = iota((BX, 128), 1)
    for z in range(NZ):
        rows = pl.ds(z // ZI * XR + z % ZI, BX, stride=ZI)
        for c in range(2):
            at = pl.multiple_of(layer * YQ + c * 128, 128)
            scratch[c, rows, :] = start[z, :, pl.ds(at, 128)]
        head = start[z, :, pl.ds(pl.multiple_of(after, 128), 128)]
        tail = start[z, :, pl.ds(pl.multiple_of(before, 128), 128)]
        head = jnp.where((lane < TURN - YQ) & (layer < VIEWS - 1), head, 0.0)
        tail = jnp.where((lane >= TURN - YQ) & (layer > 0), tail, 0.0)
        scratch[2, rows, :] = head + tail
    value = jnp.concatenate([scratch[c] for c in range(3)], axis=1)
    own[...] = value.reshape(ZG, XR, YE)
    code = to_code(value * E_SCALE).reshape(ZG, XR, YE)
    left[...] = code[:, : XR // 2]
    right[...] = code[:, XR // 2 :]


def cell(place, start):
    half = jax.ShapeDtypeStruct((ZG, XR // 2, YE), i16)
    return pl.pallas_call(
        cell_body,
        out_shape=(pltpu.VMEM((ZG, XR, YE), f32), half, half),
        in_specs=[
            pl.BlockSpec(memory_space=pltpu.SMEM),
            pl.BlockSpec(memory_space=pltpu.VMEM),
        ],
        scratch_shapes=[pltpu.VMEM((3, ROWS, 128), f32)],
        compiler_params=params(),
        cost_estimate=cost(3e6, 6e6),
    )(place, start)


def blurred_columns(field, kx, out):
    for g in range(ZG):
        x = dot(kx[...].reshape(VIEWS * XR, EXR), field[g]).astype(bf16)
        out[:, g * XR : (g + 1) * XR, :] = x.reshape(VIEWS, XR, YE)


def blurred(x, ty, bz):
    y = dot(x, ty).astype(bf16)
    return [dot(bz, columns_of(y, XR, c)) for c in range(BX // GX)]


def columns_of(rows, stride, c):
    return jnp.concatenate(
        [rows[g * stride + c * GR : g * stride + (c + 1) * GR] for g in range(ZG)], axis=0
    )


def rows_from(groups):
    return jnp.concatenate(
        [part[g * GR : (g + 1) * GR] for g in range(ZG) for part in groups], axis=0
    )


def mirrored(quotient, kxt, tyt, bzt, out, first):
    y = dot(quotient, tyt).astype(bf16)
    x = [dot(kxt, y[g * XR : (g + 1) * XR]).astype(bf16) for g in range(ZG)]
    for c in range(EX // GX):
        rows = slice(c * GR, (c + 1) * GR)
        z = dot(bzt, jnp.concatenate([part[rows] for part in x], axis=0))
        for g in range(ZG):
            part = z[g * GR : (g + 1) * GR]
            out[g, rows, :] = part if first else out[g, rows, :] + part


def quotient_of(layer, code, blur_now):
    lane = iota(code.shape, 1)
    inside = (lane < YQ) | ((lane < TURN) & (layer < VIEWS - 1)) | ((lane >= TURN) & (layer > 0))
    measured = jnp.where(inside, from_code(code) * (1.0 / M_SCALE) + M_MID, 0.0)
    return (measured / jnp.where(inside, blur_now, 1.0)).astype(bf16)


def widened(own, from_left, from_right):
    inverse = 1.0 / E_SCALE
    return jnp.concatenate(
        [from_code(from_left) * inverse, own, from_code(from_right) * inverse], axis=1
    )


def blur_body(own, from_left, from_right, kx, ty, bz, out, field, columns):
    step = pl.program_id(0)

    @pl.when(step == 0)
    def _():
        field[...] = widened(own[...], from_left[...], from_right[...]).astype(bf16)
        blurred_columns(field, kx, columns)

    out[step] = rows_from(blurred(columns[step], ty[step], bz[step]))


def blur(own, from_left, from_right, mats):
    operands = kept([own, from_left, from_right, mats[0], mats[2], mats[4]])
    return pl.pallas_call(
        blur_body,
        grid=(VIEWS,),
        out_shape=pltpu.VMEM((VIEWS, ROWS, YE), f32),
        in_specs=[KEPT] * len(operands),
        out_specs=KEPT,
        scratch_shapes=[pltpu.VMEM((ZG, EXR, YE), bf16), pltpu.VMEM((VIEWS, ROWS, YE), bf16)],
        compiler_params=params(),
        cost_estimate=cost(7e9, 1.6e7),
    )(*operands)


def joined(parts):
    return jnp.concatenate([part[...] for part in parts], axis=0)


def grouped(refs, layout):
    refs = iter(refs)
    return [[next(refs) for _ in range(n)] for n in layout]


def mirror_body(views, layout, first, last, place, *rest):
    rest = list(rest)
    before = None if first else rest.pop(0)
    codes, rest = grouped(rest, layout), rest[sum(layout) :]
    blur_ref, kxt, tyt, bzt, total = rest[:5]
    if not first:
        total[...] = before[...]
    for r, parts in zip(views, codes):
        quotient = quotient_of(place[1], joined(parts), blur_ref[r])
        mirrored(quotient, kxt[r], tyt[r], bzt[r], total, first)
    if last:
        left, right = flat(total[:, : EXR // 2]), flat(total[:, EXR // 2 :])
        send_sides(send_wide, place, rest[5], rest[6], left, right, rest[7])


def mirror(place, before, codes, views, blur_all, mats, last):
    first = before is None
    layout = tuple(len(parts) for parts in codes)
    columns = jax.ShapeDtypeStruct((wide_rows(ZG * EXR // 2), YQ), i16)
    operands = [] if first else [before]
    operands += [part for parts in codes for part in parts]
    operands = kept(operands + [blur_all, mats[1], mats[3], mats[5]])
    return pl.pallas_call(
        functools.partial(mirror_body, views, layout, first, last),
        out_shape=(pltpu.VMEM((ZG, EXR, YE), f32),) + (columns,) * (2 * last),
        in_specs=[pl.BlockSpec(memory_space=pltpu.SMEM)] + [KEPT] * len(operands),
        out_specs=(KEPT,) * (1 + 2 * last),
        scratch_shapes=[pltpu.VMEM((2,) + columns.shape, i16)] * last,
        compiler_params=params(),
        cost_estimate=cost(2e9 * len(views), 8e6 * len(views)),
    )(place, *operands)


def second_body(layout, place, own, e_left, e_right, total, x_first, x_second, *rest):
    codes, rest = grouped(rest, layout), rest[sum(layout) :]
    kx, kxt, ty, tyt, bz, bzt = rest[:6]
    estimate, center, first, second, field, columns, acc, sides, held, sent = rest[6:]
    take_sides(place, x_first, x_second, sides)
    edge = MARGIN * ZI
    middle = EXR // 2
    start = widened(own[...], e_left[...], e_right[...]) * (1.0 / VIEWS)
    for half in range(2):
        came = sides.at[half]
        rows = slice(half * middle, (half + 1) * middle)
        now = start[:, rows] * (total[:, rows] + wide_value(came).reshape(ZG, middle, YE))
        field[:, rows] = now.astype(bf16)
        inner = now[:, edge:] if half == 0 else now[:, : middle - edge]
        estimate[:, half * edge : (half + 1) * edge] = inner[:, :, :YQ]
    blurred_columns(field, kx, columns)
    for r in range(VIEWS):
        held[r] = joined(codes[r])
    acc[...] = jnp.zeros_like(acc)

    def two_views(i, _):
        for r in (2 * i, 2 * i + 1):
            blur_now = rows_from(blurred(columns[r], ty[r], bz[r]))
            quotient = quotient_of(place[1], held[r], blur_now)
            mirrored(quotient, kxt[r], tyt[r, :, :YQ], bzt[r], acc, False)
        return 0

    lax.fori_loop(0, VIEWS // 2, two_views, 0)
    center[...] = acc[:, edge : edge + XR, :]
    left, right = flat(acc[:, :edge, :]), flat(acc[:, edge + XR :, :])
    send_sides(send, place, first, second, left, right, sent)


def second(place, own, e_left, e_right, total, x_first, x_second, codes, mats):
    columns = jax.ShapeDtypeStruct((ZG * MARGIN * ZI + 16, YQ), i16)
    cell_shape = pltpu.VMEM((ZG, XR, YQ), f32)
    layout = tuple(len(parts) for parts in codes)
    operands = [own, e_left, e_right, total, x_first, x_second]
    operands += [part for parts in codes for part in parts] + list(mats)
    operands = kept(operands)
    return pl.pallas_call(
        functools.partial(second_body, layout),
        out_shape=(cell_shape, cell_shape, columns, columns),
        in_specs=[pl.BlockSpec(memory_space=pltpu.SMEM)] + [KEPT] * len(operands),
        out_specs=(KEPT,) * 4,
        scratch_shapes=[
            pltpu.VMEM((ZG, EXR, YE), bf16),
            pltpu.VMEM((VIEWS, ROWS, YE), bf16),
            pltpu.VMEM((ZG, EXR, YQ), f32),
            pltpu.VMEM((2,) + x_first.shape, i16),
            pltpu.VMEM((VIEWS, ROWS, YE), i16),
            pltpu.VMEM((2,) + columns.shape, i16),
        ],
        compiler_params=params(),
        cost_estimate=cost(1.6e10, 4e7),
    )(place, *operands)


def finish_body(place, estimate, total, x_first, x_second, low, high, sides):
    take_sides(place, x_first, x_second, sides)
    middle = XR // 2
    a = total[:, :middle] + lane_value(sides.at[0]).reshape(ZG, middle, YQ)
    b = total[:, middle:] + lane_value(sides.at[1]).reshape(ZG, middle, YQ)
    send(low, flat(estimate[:, :middle] * a * (1.0 / VIEWS)))
    send(high, flat(estimate[:, middle:] * b * (1.0 / VIEWS)))


def finish(place, estimate, total, x_first, x_second):
    half = jax.ShapeDtypeStruct((ROWS // 2 + 16, YQ), i16)
    return pl.pallas_call(
        finish_body,
        out_shape=(half, half),
        in_specs=[pl.BlockSpec(memory_space=pltpu.SMEM)] + [KEPT] * 4,
        out_specs=(KEPT, KEPT),
        scratch_shapes=[pltpu.VMEM((2,) + x_first.shape, i16)],
        compiler_params=params(),
        cost_estimate=cost(5e6, 4e6),
    )(place, *kept([estimate, total, x_first, x_second]))


def spread_out(codes, scratch, store):
    middle = XR // 2
    for half in range(2):
        value = lane_value(codes[half])
        for c in range(2):
            scratch[half, c] = value[:, c * 128 : (c + 1) * 128]
            for z in range(NZ):
                rows = pl.ds(z // ZI * middle + z % ZI, BX // 2, stride=ZI)
                store(z, half, c, scratch[half, c, rows, :])


def gather_body(place, *rest):
    codes, out, scratch = rest[: 2 * VIEWS - 2], rest[2 * VIEWS - 2], rest[2 * VIEWS - 1]
    for i, r in enumerate((0, 1, 3)):
        at = lax.rem(place[1] + VIEWS - r, VIEWS) * YQ

        def store(z, half, c, value):
            lanes = pl.ds(pl.multiple_of(at + c * 128, 128), 128)
            out[z, half * BX // 2 : (half + 1) * BX // 2, lanes] = value

        spread_out(codes[2 * i : 2 * i + 2], scratch.at[i], store)


def gathered(place, codes):
    return pl.pallas_call(
        gather_body,
        out_shape=jax.ShapeDtypeStruct((NZ, BX, VIEWS * YQ), f32),
        in_specs=[pl.BlockSpec(memory_space=pltpu.SMEM)] + [KEPT] * len(codes),
        scratch_shapes=[pltpu.VMEM((VIEWS - 1, 2, 2, ROWS // 2, 128), f32)],
        compiler_params=params(),
        cost_estimate=cost(3e6, 6e6),
    )(place, *kept(codes))


def complete_body(place, low, high, _, out, scratch, quarter, sem):
    def store(z, half, c, value):
        quarter[z, half * BX // 2 : (half + 1) * BX // 2, c * 128 : (c + 1) * 128] = value

    spread_out((low, high), scratch, store)
    at = pl.multiple_of(lax.rem(place[1] + 2, VIEWS) * YQ, YQ)
    move = pltpu.make_async_copy(quarter, out.at[:, :, pl.ds(at, YQ)], sem)
    move.start()
    move.wait()


def completed(place, low, high, out):
    anywhere = pl.BlockSpec(memory_space=pl.ANY)
    vmem = pl.BlockSpec(memory_space=pltpu.VMEM)
    return pl.pallas_call(
        complete_body,
        out_shape=jax.ShapeDtypeStruct(out.shape, f32),
        in_specs=[pl.BlockSpec(memory_space=pltpu.SMEM), vmem, vmem, anywhere],
        out_specs=anywhere,
        input_output_aliases={3: 0},
        scratch_shapes=[
            pltpu.VMEM((2, 2, ROWS // 2, 128), f32),
            pltpu.VMEM((NZ, BX, YQ), f32),
            pltpu.SemaphoreType.DMA,
        ],
        compiler_params=params(),
        cost_estimate=cost(1e6, 2e6),
    )(place, *kept([low, high]), out)


def per_device(view_tiles, route_block, route_column, psf_taps, start_estimate):
    groups = lax.axis_size("block")
    cap = max(2, (2 * BX + groups - 1) // groups)
    me, layer = lax.axis_index("block"), lax.axis_index("view")
    place = jnp.stack([me, layer]).astype(i32)

    def around(x, shift):
        return lax.ppermute(x, "view", [(i, (i + shift) % VIEWS) for i in range(VIEWS)])

    def shifted(x, shift):
        pairs = [(i, i + shift) for i in range(groups) if 0 <= i + shift < groups]
        return lax.ppermute(x, "block", pairs)

    def swapped(x, start):
        pairs = []
        for i in range(start, groups - 1, 2):
            pairs += [(i, i + 1), (i + 1, i)]
        return lax.ppermute(x, "block", pairs) if pairs else jnp.zeros_like(x)

    outgoing = pack(cap, groups, route_block[0], route_column[0], view_tiles[0])
    arrived = lax.all_to_all(outgoing, "block", split_axis=0, concat_axis=0, tiled=True)

    psf, start_estimate, _ = lax.optimization_barrier((psf_taps[0], start_estimate, outgoing))
    kernel = psf / jnp.sum(psf, axis=1, keepdims=True)
    kernel = kernel.astype(bf16).astype(f32)
    taps = [kernel] + [around(kernel, r) for r in range(1, VIEWS)]
    own, to_left, to_right = cell(place, start_estimate)
    e_left, e_right = shifted(to_right, 1), shifted(to_left, -1)

    codes = unpack(cap, place, arrived)
    own, taps, codes = lax.optimization_barrier((own, taps, codes))
    low_on, high_on = around(codes[2], 1), around(codes[3], -1)
    codes = [
        [codes[0]],
        [around(codes[1], 1)],
        [around(low_on, 1), around(high_on, -1)],
        [around(codes[4], -1)],
    ]
    mats = bands(jnp.stack(taps).reshape(VIEWS, 3 * TAPS))
    blur_all = blur(own, e_left, e_right, mats)
    (total,) = mirror(place, None, codes[:1], [0], blur_all, mats, False)
    (total,) = mirror(place, total, [codes[1], codes[3]], [1, 3], blur_all, mats, False)
    total, first, second_part = mirror(place, total, codes[2:3], [2], blur_all, mats, True)
    x_first, x_second = swapped(first, 1), swapped(second_part, 0)
    estimate, center, first, second_part = second(
        place, own, e_left, e_right, total, x_first, x_second, codes, mats
    )
    x_first, x_second = swapped(first, 1), swapped(second_part, 0)
    low, high = finish(place, estimate, center, x_first, x_second)
    low_after, high_before = around(low, -1), around(high, 1)
    high_after, low_before = around(high, -1), around(low, 1)
    low_across, high_across = around(low_after, -1), around(high_before, 1)
    out = gathered(place, [low, high, low_before, high_before, low_after, high_after])
    return completed(place, low_across, high_across, out)


def solution(mesh):
    placed = (
        P("view", "block", None, None),
        P("view", "block"),
        P("view", "block"),
        P("view", None, None),
        P(None, "block", None),
    )
    return jax.shard_map(
        per_device, mesh=mesh, in_specs=placed, out_specs=P(None, "block", None), check_vma=False
    )
```

profile of v0, /device:TPU:11, one launch (start us, length us, event | category | flops | bytes accessed | tf_op | source)
XLA Modules:
  0.0 239.9 jit_solution(1350307743335410699)
XLA Ops:
  0.0 5.8 %shard_map.55 = bf16[64,400,128]{2,1,0:T(8,128)(2,1)} custom-call(s32[80]{0:T(128)} %bitcast.11, s32[80]{0:T(128)} %bitcast.12, bf16[80,24,1024]{2,1,0:T(8,128)(2,1)} %bitcast.8), custom_call_target="tpu_custom_call" | custom-call | bytes 7864320 | tf_op jit(solution)/shard_map/pallas_call | solution.py:247
  5.8 0.0 copy-start.5
  5.9 0.0 copy-start
  5.9 10.0 %all-to-all-start = ((bf16[64,400,128]{2,1,0:T(8,128)(2,1)}), bf16[64,400,128]{2,1,0:T(8,128)(2,1)}, u32[]{:S(2)}, u32[]{:S(2)}) async-start(bf16[64,400,128]{2,1,0:T(8,128)(2,1)} %shard_map.55), calls=%async_computation | async-start | bytes 13107200 | tf_op jit(solution)/shard_map/all_to_all | solution.py:748
  15.9 0.1 reduce_sum.9
  16.0 0.1 fusion
  16.1 5.1 %collective-permute-start.2 = (f32[3,31]{1,0:T(4,128)S(1)}, f32[3,31]{1,0:T(4,128)S(1)}, u32[]{:S(2)}, u32[]{:S(2)}) collective-permute-start(f32[3,31]{1,0:T(4,128)S(1)} %fusion), channel_id=1, source_target_pairs={{0,192},{64,0},{128,64},{192,128},{1,193},{65,1},{129,65},{193,129... | collective-permute-start | bytes 1124 | tf_op jit(solution)/shard_map/ppermute | solution.py:735
  21.3 1.2 collective-permute-start.1
  22.4 2.1 collective-permute-start
  24.5 0.1 pad_add_fusion.place
  24.6 2.1 shard_map.56
  26.6 1.0 copy-done.1
  27.7 4.2 %collective-permute-start.3 = (s16[3,128,384]{2,1,0:T(8,128)(2,1)}, s16[3,128,384]{2,1,0:T(8,128)(2,1)S(1)}, u32[]{:S(2)}, u32[]{:S(2)}) collective-permute-start(s16[3,128,384]{2,1,0:T(8,128)(2,1)} %get-tuple-element.49), channel_id=1, source_target_pairs={{0,1},{1,2},{2,3},{3,4},{4,5},{5,6},{6,7},{7,8},{8,9},{9,10},{10,1... | collective-permute-start | bytes 884744 | tf_op jit(solution)/shard_map/ppermute | solution.py:739
  31.8 1.9 collective-permute-start.4
  33.8 66.0 %all-to-all-done.arrived.whole_arrived = bf16[64,400,128]{2,1,0:T(8,128)(2,1)} async-done(((bf16[64,400,128]{2,1,0:T(8,128)(2,1)}), bf16[64,400,128]{2,1,0:T(8,128)(2,1)}, u32[]{:S(2)}, u32[]{:S(2)}) %all-to-all-start) | async-done | bytes 6553632 | tf_op jit(solution)/shard_map/all_to_all | solution.py:748
  99.7 7.9 %shard_map.57 = (s16[768,384]{1,0:T(8,128)(2,1)S(1)}, s16[768,384]{1,0:T(8,128)(2,1)S(1)}, s16[384,384]{1,0:T(8,128)(2,1)S(1)}, s16[384,384]{1,0:T(8,128)(2,1)S(1)}, s16[768,384]{1,0:T(8,128)(2,1)S(1)}) custom-call(s32[2]{0:T(128)S(1)} %pad_add_fusion.place, bf16[64,400,128]{2,1,0:T(8,128)(2,1)} %all-to-all-done.arrived.whole_arrived, ...), custom_call_target="tpu_custom_call" | custom-call | flops 3276800 | bytes 6553600 | tf_op jit(solution)/shard_map/pallas_call | solution.py:352
  107.6 0.0 collective-permute-done.2
  107.7 0.0 collective-permute-done.1
  107.7 0.0 collective-permute-done
  107.7 0.1 stack.27
  107.8 0.1 stack.28
  107.8 0.1 stack.29
  107.9 0.1 stack.30
  108.0 2.6 %collective-permute-start.7 = (s16[384,384]{1,0:T(8,128)(2,1)S(1)}, s16[384,384]{1,0:T(8,128)(2,1)S(1)}, u32[]{:S(2)}, u32[]{:S(2)}) collective-permute-start(s16[384,384]{1,0:T(8,128)(2,1)S(1)} %get-tuple-element.64), channel_id=1, source_target_pairs={{0,64},{64,128},{128,192},{192,0},{1,65},{65,129},{129,193},{193,1... | collective-permute-start | bytes 884744 | tf_op jit(solution)/shard_map/ppermute | solution.py:735
  110.6 2.0 collective-permute-start.9
  112.6 0.8 collective-permute-start.5
  113.4 0.0 copy-start.2
  113.5 5.3 %shard_map.58 = (bf16[4,256,512]{2,1,0:T(8,128)(2,1)S(1)}, bf16[4,512,256]{2,1,0:T(8,128)(2,1)S(1)}, bf16[4,384,384]{2,1,0:T(8,128)(2,1)S(1)}, bf16[4,384,384]{2...) custom-call(f32[4,93]{1,0:T(4,128)S(1)} %pad_maximum_fusion.taps), custom_call_target="tpu_custom_call" | custom-call | flops 4000000000 | bytes 20000000 | tf_op jit(solution)/shard_map/pallas_call | solution.py:420
  118.7 0.0 collective-permute-done.3.from_left.e_left
  118.7 3.0 %collective-permute-start.6 = (s16[768,384]{1,0:T(8,128)(2,1)S(1)}, s16[768,384]{1,0:T(8,128)(2,1)S(1)}, u32[]{:S(2)}, u32[]{:S(2)}) collective-permute-start(s16[768,384]{1,0:T(8,128)(2,1)S(1)} %get-tuple-element.63), channel_id=1, source_target_pairs={{0,192},{64,0},{128,64},{192,128},{1,193},{65,1},{129,65},{193,129... | collective-permute-start | bytes 1769480 | tf_op jit(solution)/shard_map/ppermute | solution.py:735
  121.7 0.0 collective-permute-done.4.from_right.e_right
  121.8 5.5 %shard_map.59.rest_1_.rest_3_ = f32[4,768,384]{2,1,0:T(8,128)S(1)} custom-call(f32[3,256,384]{2,1,0:T(8,128)S(1)} %copy-done.2, s16[3,128,384]{2,1,0:T(8,128)(2,1)S(1)} %collective-permute-done.3.from_left.e_left, s16[3,128,384]{2,1,0:T(8,128)(2,1)S(1)} %collective-permute-done.4.from_right.e_right, bf16[4,256,512]{2,1,0:T(8,128)(2,1)S(1)} %get-tuple-element.56.kx.rest_5_, ...), custom_call_target="tpu_custom_call" | custom-call | flops 7000000000 | bytes 16000000 | tf_op jit(solution)/shard_map/pallas_call | solution.py:530
  127.3 2.0 shard_map.60.rest_0_
  129.3 0.0 collective-permute-done.7
  129.3 0.9 collective-permute-start.8
  130.2 0.0 collective-permute-done.9
  130.2 2.7 %collective-permute-start.10 = (s16[384,384]{1,0:T(8,128)(2,1)S(1)}, s16[384,384]{1,0:T(8,128)(2,1)S(1)}, u32[]{:S(2)}, u32[]{:S(2)}) collective-permute-start(s16[384,384]{1,0:T(8,128)(2,1)S(1)} %collective-permute-done.9), channel_id=1, source_target_pairs={{0,192},{64,0},{128,64},{192,128},{1,193},{65,1},{129,65},{193,129... | collective-permute-start | bytes 884744 | tf_op jit(solution)/shard_map/ppermute | solution.py:735
  132.9 0.0 collective-permute-done.5.rest_1_
  132.9 22.0 %collective-permute-done.6.rest_2_.rest_4_ = s16[768,384]{1,0:T(8,128)(2,1)S(1)} collective-permute-done((s16[768,384]{1,0:T(8,128)(2,1)S(1)}, s16[768,384]{1,0:T(8,128)(2,1)S(1)}, u32[]{:S(2)}, u32[]{:S(2)}) %collective-permute-start.6) | collective-permute-done | bytes 589856 | tf_op jit(solution)/shard_map/ppermute | solution.py:735
  155.0 3.2 %shard_map.61.rest_0_ = f32[3,512,384]{2,1,0:T(8,128)S(1)} custom-call(s32[2]{0:T(128)S(1)} %pad_add_fusion.place, f32[3,512,384]{2,1,0:T(8,128)S(1)} %shard_map.60.rest_0_, s16[768,384]{1,0:T(8,128)(2,1)S(1)} %collective-permute-done.5.rest_1_, s16[768,384]{1,0:T(8,128)(2,1)S(1)} %collective-permute-done.6.rest_2_.rest_4_, ...), custom_call_target="tpu_custom_call" | custom-call | flops 4000000000 | bytes 16000000 | tf_op jit(solution)/shard_map/pallas_call | solution.py:573
  158.2 7.0 %collective-permute-done.8.rest_1_.rest_2_ = s16[384,384]{1,0:T(8,128)(2,1)S(1)} collective-permute-done((s16[384,384]{1,0:T(8,128)(2,1)S(1)}, s16[384,384]{1,0:T(8,128)(2,1)S(1)}, u32[]{:S(2)}, u32[]{:S(2)}) %collective-permute-start.8) | collective-permute-done | bytes 294944 | tf_op jit(solution)/shard_map/ppermute | solution.py:735
  165.2 2.7 %shard_map.62 = (f32[3,512,384]{2,1,0:T(8,128)S(1)}, s16[992,256]{1,0:T(8,128)(2,1)S(1)}, s16[992,256]{1,0:T(8,128)(2,1)S(1)}) custom-call(s32[2]{0:T(128)S(1)} %pad_add_fusion.place, f32[3,512,384]{2,1,0:T(8,128)S(1)} %shard_map.61.rest_0_, s16[384,384]{1,0:T(8,128)(2,1)S(1)} %collective-permute-done.8.rest_1_.rest_2_, ...), custom_call_target="tpu_custom_call" | custom-call | flops 2000000000 | bytes 8000000 | tf_op jit(solution)/shard_map/pallas_call | solution.py:573
  167.8 5.3 %collective-permute-start.11 = (s16[992,256]{1,0:T(8,128)(2,1)S(1)}, s16[992,256]{1,0:T(8,128)(2,1)S(1)}, u32[]{:S(2)}, u32[]{:S(2)}) collective-permute-start(s16[992,256]{1,0:T(8,128)(2,1)S(1)} %get-tuple-element.67), channel_id=1, source_target_pairs={{1,2},{2,1},{3,4},{4,3},{5,6},{6,5},{7,8},{8,7},{9,10},{10,9},{11,... | collective-permute-start | bytes 1523720 | tf_op jit(solution)/shard_map/ppermute | solution.py:745
  173.2 0.1 collective-permute-start.12
  173.3 11.4 %collective-permute-done.11.x_first = s16[992,256]{1,0:T(8,128)(2,1)S(1)} collective-permute-done((s16[992,256]{1,0:T(8,128)(2,1)S(1)}, s16[992,256]{1,0:T(8,128)(2,1)S(1)}, u32[]{:S(2)}, u32[]{:S(2)}) %collective-permute-start.11) | collective-permute-done | bytes 507936 | tf_op jit(solution)/shard_map/ppermute | solution.py:745
  184.6 0.0 collective-permute-done.12.x_second
  184.6 10.6 %shard_map.63 = (f32[3,256,256]{2,1,0:T(8,128)S(1)}, f32[3,256,256]{2,1,0:T(8,128)S(1)}, s16[400,256]{1,0:T(8,128)(2,1)S(1)}, s16[400,256]{1,0:T(8,128)(2,1)S(1)}) custom-call(s32[2]{0:T(128)S(1)} %pad_add_fusion.place, f32[3,256,384]{2,1,0:T(8,128)S(1)} %copy-done.2, s16[3,128,384]{2,1,0:T(8,128)(2,1)S(1)} %collective-permute-done.3.from_left.e_left, ...), custom_call_target="tpu_custom_call" | custom-call | flops 16000000000 | bytes 40000000 | tf_op jit(solution)/shard_map/pallas_call | solution.py:624
  195.2 2.3 collective-permute-start.13
  197.5 0.1 collective-permute-start.14
  197.6 6.2 %collective-permute-done.13.x_first = s16[400,256]{1,0:T(8,128)(2,1)S(1)} collective-permute-done((s16[400,256]{1,0:T(8,128)(2,1)S(1)}, s16[400,256]{1,0:T(8,128)(2,1)S(1)}, u32[]{:S(2)}, u32[]{:S(2)}) %collective-permute-start.13) | collective-permute-done | bytes 204832 | tf_op jit(solution)/shard_map/ppermute | solution.py:745
  203.8 0.0 collective-permute-done.14.x_second
  203.8 1.0 shard_map.64
  204.8 3.2 %collective-permute-start.15 = (s16[400,256]{1,0:T(8,128)(2,1)S(1)}, s16[400,256]{1,0:T(8,128)(2,1)S(1)}, u32[]{:S(2)}, u32[]{:S(2)}) collective-permute-start(s16[400,256]{1,0:T(8,128)(2,1)S(1)} %get-tuple-element.73.rest_0_), channel_id=1, source_target_pairs={{0,192},{64,0},{128,64},{192,128},{1,193},{65,1},{129,65},{193,129... | collective-permute-start | bytes 614408 | tf_op jit(solution)/shard_map/ppermute | solution.py:735
  208.0 3.6 %collective-permute-start.20 = (s16[400,256]{1,0:T(8,128)(2,1)S(1)}, s16[400,256]{1,0:T(8,128)(2,1)S(1)}, u32[]{:S(2)}, u32[]{:S(2)}) collective-permute-start(s16[400,256]{1,0:T(8,128)(2,1)S(1)} %get-tuple-element.74.rest_1_), channel_id=1, source_target_pairs={{0,192},{64,0},{128,64},{192,128},{1,193},{65,1},{129,65},{193,129... | collective-permute-start | bytes 614408 | tf_op jit(solution)/shard_map/ppermute | solution.py:735
  211.6 3.7 %collective-permute-done.15.rest_4_ = s16[400,256]{1,0:T(8,128)(2,1)S(1)} collective-permute-done((s16[400,256]{1,0:T(8,128)(2,1)S(1)}, s16[400,256]{1,0:T(8,128)(2,1)S(1)}, u32[]{:S(2)}, u32[]{:S(2)}) %collective-permute-start.15) | collective-permute-done | bytes 204832 | tf_op jit(solution)/shard_map/ppermute | solution.py:735
  215.3 4.3 %collective-permute-start.16 = (s16[400,256]{1,0:T(8,128)(2,1)S(1)}, s16[400,256]{1,0:T(8,128)(2,1)S(1)}, u32[]{:S(2)}, u32[]{:S(2)}) collective-permute-start(s16[400,256]{1,0:T(8,128)(2,1)S(1)} %collective-permute-done.15.rest_4_), channel_id=1, source_target_pairs={{0,192},{64,0},{128,64},{192,128},{1,193},{65,1},{129,65},{193,129... | collective-permute-start | bytes 614408 | tf_op jit(solution)/shard_map/ppermute | solution.py:735
  219.5 0.0 collective-permute-done.17.rest_3_
  219.6 0.0 collective-permute-start.18
  219.6 14.9 %collective-permute-done.19.rest_2_ = s16[400,256]{1,0:T(8,128)(2,1)S(1)} collective-permute-done((s16[400,256]{1,0:T(8,128)(2,1)S(1)}, s16[400,256]{1,0:T(8,128)(2,1)S(1)}, u32[]{:S(2)}, u32[]{:S(2)}) %collective-permute-start.19) | collective-permute-done | bytes 204832 | tf_op jit(solution)/shard_map/ppermute | solution.py:735
  234.5 0.0 collective-permute-done.20.rest_5_
  234.5 3.0 %shard_map.65._ = f32[24,32,1024]{2,1,0:T(8,128)} custom-call(s32[2]{0:T(128)S(1)} %pad_add_fusion.place, s16[400,256]{1,0:T(8,128)(2,1)S(1)} %get-tuple-element.73.rest_0_, s16[400,256]{1,0:T(8,128)(2,1)S(1)} %get-tuple-element.74.rest_1_, s16[400,256]{1,0:T(8,128)(2,1)S(1)} %collective-permute-done.19.rest_2_, ...), custom_call_target="tpu_custom_call" | custom-call | flops 3000000 | bytes 6000000 | tf_op jit(solution)/shard_map/pallas_call | solution.py:688
  237.4 0.0 collective-permute-done.16.low
  237.4 0.6 collective-permute-done.18.high
  238.0 1.7 shard_map.66
  (13 shorter events, 0.0 us)
Async XLA Ops:
  5.8 10.1 %copy-start.5 = (f32[1,3,31]{2,0,1:T(1,128)S(1)}, f32[1,3,31]{2,0,1:T(1,128)}, u32[]{:S(2)}) copy-start(f32[1,3,31]{2,0,1:T(1,128)} %param.8) | copy-start | bytes 1120
  5.9 18.7 %copy-start = (f32[24,32,1024]{2,1,0:T(8,128)S(1)}, f32[24,32,1024]{2,1,0:T(8,128)}, u32[]{:S(2)}) copy-start(f32[24,32,1024]{2,1,0:T(8,128)} %start) | copy-start | bytes 9437188
  5.9 93.9 %all-to-all-start = ((bf16[64,400,128]{2,1,0:T(8,128)(2,1)}), bf16[64,400,128]{2,1,0:T(8,128)(2,1)}, u32[]{:S(2)}, u32[]{:S(2)}) async-start(bf16[64,400,128]{2,1,0:T(8,128)(2,1)} %shard_map.55), calls=%async_computation | async-start | bytes 13107200 | tf_op jit(solution)/shard_map/all_to_all | solution.py:748
  16.1 91.5 %collective-permute-start.2 = (f32[3,31]{1,0:T(4,128)S(1)}, f32[3,31]{1,0:T(4,128)S(1)}, u32[]{:S(2)}, u32[]{:S(2)}) collective-permute-start(f32[3,31]{1,0:T(4,128)S(1)} %fusion), channel_id=1, source_target_pairs={{0,192},{64,0},{128,64},{192,128},{1,193},{65,1},{129,65},{193,129... | collective-permute-start | bytes 1124 | tf_op jit(solution)/shard_map/ppermute | solution.py:735
  21.3 86.4 %collective-permute-start.1 = (f32[3,31]{1,0:T(4,128)S(1)}, f32[3,31]{1,0:T(4,128)S(1)}, u32[]{:S(2)}, u32[]{:S(2)}) collective-permute-start(f32[3,31]{1,0:T(4,128)S(1)} %fusion), channel_id=1, source_target_pairs={{0,128},{64,192},{128,0},{192,64},{1,129},{65,193},{129,1},{193,65... | collective-permute-start | bytes 1124 | tf_op jit(solution)/shard_map/ppermute | solution.py:735
  22.4 85.2 %collective-permute-start = (f32[3,31]{1,0:T(4,128)S(1)}, f32[3,31]{1,0:T(4,128)S(1)}, u32[]{:S(2)}, u32[]{:S(2)}) collective-permute-start(f32[3,31]{1,0:T(4,128)S(1)} %fusion), channel_id=1, source_target_pairs={{0,64},{64,128},{128,192},{192,0},{1,65},{65,129},{129,193},{193,1... | collective-permute-start | bytes 1124 | tf_op jit(solution)/shard_map/ppermute | solution.py:735
  26.6 1.0 copy-start.1
  27.7 91.1 %collective-permute-start.3 = (s16[3,128,384]{2,1,0:T(8,128)(2,1)}, s16[3,128,384]{2,1,0:T(8,128)(2,1)S(1)}, u32[]{:S(2)}, u32[]{:S(2)}) collective-permute-start(s16[3,128,384]{2,1,0:T(8,128)(2,1)} %get-tuple-element.49), channel_id=1, source_target_pairs={{0,1},{1,2},{2,3},{3,4},{4,5},{5,6},{6,7},{7,8},{8,9},{9,10},{10,1... | collective-permute-start | bytes 884744 | tf_op jit(solution)/shard_map/ppermute | solution.py:739
  31.8 89.9 %collective-permute-start.4 = (s16[3,128,384]{2,1,0:T(8,128)(2,1)}, s16[3,128,384]{2,1,0:T(8,128)(2,1)S(1)}, u32[]{:S(2)}, u32[]{:S(2)}) collective-permute-start(s16[3,128,384]{2,1,0:T(8,128)(2,1)} %get-tuple-element.50), channel_id=1, source_target_pairs={{1,0},{2,1},{3,2},{4,3},{5,4},{6,5},{7,6},{8,7},{9,8},{10,9},{11,1... | collective-permute-start | bytes 884744 | tf_op jit(solution)/shard_map/ppermute | solution.py:739
  108.0 21.3 %collective-permute-start.7 = (s16[384,384]{1,0:T(8,128)(2,1)S(1)}, s16[384,384]{1,0:T(8,128)(2,1)S(1)}, u32[]{:S(2)}, u32[]{:S(2)}) collective-permute-start(s16[384,384]{1,0:T(8,128)(2,1)S(1)} %get-tuple-element.64), channel_id=1, source_target_pairs={{0,64},{64,128},{128,192},{192,0},{1,65},{65,129},{129,193},{193,1... | collective-permute-start | bytes 884744 | tf_op jit(solution)/shard_map/ppermute | solution.py:735
  110.6 19.6 %collective-permute-start.9 = (s16[384,384]{1,0:T(8,128)(2,1)S(1)}, s16[384,384]{1,0:T(8,128)(2,1)S(1)}, u32[]{:S(2)}, u32[]{:S(2)}) collective-permute-start(s16[384,384]{1,0:T(8,128)(2,1)S(1)} %get-tuple-element.65), channel_id=1, source_target_pairs={{0,192},{64,0},{128,64},{192,128},{1,193},{65,1},{129,65},{193,129... | collective-permute-start | bytes 884744 | tf_op jit(solution)/shard_map/ppermute | solution.py:735
  112.6 20.3 %collective-permute-start.5 = (s16[768,384]{1,0:T(8,128)(2,1)S(1)}, s16[768,384]{1,0:T(8,128)(2,1)S(1)}, u32[]{:S(2)}, u32[]{:S(2)}) collective-permute-start(s16[768,384]{1,0:T(8,128)(2,1)S(1)} %get-tuple-element.62), channel_id=1, source_target_pairs={{0,64},{64,128},{128,192},{192,0},{1,65},{65,129},{129,193},{193,1... | collective-permute-start | bytes 1769480 | tf_op jit(solution)/shard_map/ppermute | solution.py:735
  113.4 8.3 %copy-start.2 = (f32[3,256,384]{2,1,0:T(8,128)S(1)}, f32[3,256,384]{2,1,0:T(8,128)}, u32[]{:S(2)}) copy-start(f32[3,256,384]{2,1,0:T(8,128)} %copy-done.1) | copy-start | bytes 3538948
  118.7 36.3 %collective-permute-start.6 = (s16[768,384]{1,0:T(8,128)(2,1)S(1)}, s16[768,384]{1,0:T(8,128)(2,1)S(1)}, u32[]{:S(2)}, u32[]{:S(2)}) collective-permute-start(s16[768,384]{1,0:T(8,128)(2,1)S(1)} %get-tuple-element.63), channel_id=1, source_target_pairs={{0,192},{64,0},{128,64},{192,128},{1,193},{65,1},{129,65},{193,129... | collective-permute-start | bytes 1769480 | tf_op jit(solution)/shard_map/ppermute | solution.py:735
  121.7 5.5 %copy-start.3 = (s16[3,128,384]{2,1,0:T(8,128)(2,1)}, s16[3,128,384]{2,1,0:T(8,128)(2,1)S(1)}, u32[]{:S(2)}) copy-start(s16[3,128,384]{2,1,0:T(8,128)(2,1)S(1)} %collective-permute-done.4.from_right.e_right) | copy-start | bytes 884740
  129.3 35.9 %collective-permute-start.8 = (s16[384,384]{1,0:T(8,128)(2,1)S(1)}, s16[384,384]{1,0:T(8,128)(2,1)S(1)}, u32[]{:S(2)}, u32[]{:S(2)}) collective-permute-start(s16[384,384]{1,0:T(8,128)(2,1)S(1)} %collective-permute-done.7), channel_id=1, source_target_pairs={{0,64},{64,128},{128,192},{192,0},{1,65},{65,129},{129,193},{193,1... | collective-permute-start | bytes 884744 | tf_op jit(solution)/shard_map/ppermute | solution.py:735
  130.2 34.9 %collective-permute-start.10 = (s16[384,384]{1,0:T(8,128)(2,1)S(1)}, s16[384,384]{1,0:T(8,128)(2,1)S(1)}, u32[]{:S(2)}, u32[]{:S(2)}) collective-permute-start(s16[384,384]{1,0:T(8,128)(2,1)S(1)} %collective-permute-done.9), channel_id=1, source_target_pairs={{0,192},{64,0},{128,64},{192,128},{1,193},{65,1},{129,65},{193,129... | collective-permute-start | bytes 884744 | tf_op jit(solution)/shard_map/ppermute | solution.py:735
  158.2 26.4 %copy-start.4 = (s16[3,128,384]{2,1,0:T(8,128)(2,1)S(1)}, s16[3,128,384]{2,1,0:T(8,128)(2,1)}, u32[]{:S(2)}) copy-start(s16[3,128,384]{2,1,0:T(8,128)(2,1)} %copy-done.3) | copy-start | bytes 884740
  167.8 16.8 %collective-permute-start.11 = (s16[992,256]{1,0:T(8,128)(2,1)S(1)}, s16[992,256]{1,0:T(8,128)(2,1)S(1)}, u32[]{:S(2)}, u32[]{:S(2)}) collective-permute-start(s16[992,256]{1,0:T(8,128)(2,1)S(1)} %get-tuple-element.67), channel_id=1, source_target_pairs={{1,2},{2,1},{3,4},{4,3},{5,6},{6,5},{7,8},{8,7},{9,10},{10,9},{11,... | collective-permute-start | bytes 1523720 | tf_op jit(solution)/shard_map/ppermute | solution.py:745
  173.2 11.5 %collective-permute-start.12 = (s16[992,256]{1,0:T(8,128)(2,1)S(1)}, s16[992,256]{1,0:T(8,128)(2,1)S(1)}, u32[]{:S(2)}, u32[]{:S(2)}) collective-permute-start(s16[992,256]{1,0:T(8,128)(2,1)S(1)} %get-tuple-element.68), channel_id=1, source_target_pairs={{0,1},{1,0},{2,3},{3,2},{4,5},{5,4},{6,7},{7,6},{8,9},{9,8},{10,11... | collective-permute-start | bytes 1523720 | tf_op jit(solution)/shard_map/ppermute | solution.py:745
  195.2 8.6 %collective-permute-start.13 = (s16[400,256]{1,0:T(8,128)(2,1)S(1)}, s16[400,256]{1,0:T(8,128)(2,1)S(1)}, u32[]{:S(2)}, u32[]{:S(2)}) collective-permute-start(s16[400,256]{1,0:T(8,128)(2,1)S(1)} %get-tuple-element.71), channel_id=1, source_target_pairs={{1,2},{2,1},{3,4},{4,3},{5,6},{6,5},{7,8},{8,7},{9,10},{10,9},{11,... | collective-permute-start | bytes 614408 | tf_op jit(solution)/shard_map/ppermute | solution.py:745
  197.5 6.3 %collective-permute-start.14 = (s16[400,256]{1,0:T(8,128)(2,1)S(1)}, s16[400,256]{1,0:T(8,128)(2,1)S(1)}, u32[]{:S(2)}, u32[]{:S(2)}) collective-permute-start(s16[400,256]{1,0:T(8,128)(2,1)S(1)} %get-tuple-element.72), channel_id=1, source_target_pairs={{0,1},{1,0},{2,3},{3,2},{4,5},{5,4},{6,7},{7,6},{8,9},{9,8},{10,11... | collective-permute-start | bytes 614408 | tf_op jit(solution)/shard_map/ppermute | solution.py:745
  204.8 10.5 %collective-permute-start.15 = (s16[400,256]{1,0:T(8,128)(2,1)S(1)}, s16[400,256]{1,0:T(8,128)(2,1)S(1)}, u32[]{:S(2)}, u32[]{:S(2)}) collective-permute-start(s16[400,256]{1,0:T(8,128)(2,1)S(1)} %get-tuple-element.73.rest_0_), channel_id=1, source_target_pairs={{0,192},{64,0},{128,64},{192,128},{1,193},{65,1},{129,65},{193,129... | collective-permute-start | bytes 614408 | tf_op jit(solution)/shard_map/ppermute | solution.py:735
  208.0 11.6 %collective-permute-start.17 = (s16[400,256]{1,0:T(8,128)(2,1)S(1)}, s16[400,256]{1,0:T(8,128)(2,1)S(1)}, u32[]{:S(2)}, u32[]{:S(2)}) collective-permute-start(s16[400,256]{1,0:T(8,128)(2,1)S(1)} %get-tuple-element.74.rest_1_), channel_id=1, source_target_pairs={{0,64},{64,128},{128,192},{192,0},{1,65},{65,129},{129,193},{193,1... | collective-permute-start | bytes 614408 | tf_op jit(solution)/shard_map/ppermute | solution.py:735
  208.0 26.5 %collective-permute-start.19 = (s16[400,256]{1,0:T(8,128)(2,1)S(1)}, s16[400,256]{1,0:T(8,128)(2,1)S(1)}, u32[]{:S(2)}, u32[]{:S(2)}) collective-permute-start(s16[400,256]{1,0:T(8,128)(2,1)S(1)} %get-tuple-element.73.rest_0_), channel_id=1, source_target_pairs={{0,64},{64,128},{128,192},{192,0},{1,65},{65,129},{129,193},{193,1... | collective-permute-start | bytes 614408 | tf_op jit(solution)/shard_map/ppermute | solution.py:735
  208.0 26.5 %collective-permute-start.20 = (s16[400,256]{1,0:T(8,128)(2,1)S(1)}, s16[400,256]{1,0:T(8,128)(2,1)S(1)}, u32[]{:S(2)}, u32[]{:S(2)}) collective-permute-start(s16[400,256]{1,0:T(8,128)(2,1)S(1)} %get-tuple-element.74.rest_1_), channel_id=1, source_target_pairs={{0,192},{64,0},{128,64},{192,128},{1,193},{65,1},{129,65},{193,129... | collective-permute-start | bytes 614408 | tf_op jit(solution)/shard_map/ppermute | solution.py:735
  215.3 22.1 %collective-permute-start.16 = (s16[400,256]{1,0:T(8,128)(2,1)S(1)}, s16[400,256]{1,0:T(8,128)(2,1)S(1)}, u32[]{:S(2)}, u32[]{:S(2)}) collective-permute-start(s16[400,256]{1,0:T(8,128)(2,1)S(1)} %collective-permute-done.15.rest_4_), channel_id=1, source_target_pairs={{0,192},{64,0},{128,64},{192,128},{1,193},{65,1},{129,65},{193,129... | collective-permute-start | bytes 614408 | tf_op jit(solution)/shard_map/ppermute | solution.py:735
  219.6 18.5 %collective-permute-start.18 = (s16[400,256]{1,0:T(8,128)(2,1)S(1)}, s16[400,256]{1,0:T(8,128)(2,1)S(1)}, u32[]{:S(2)}, u32[]{:S(2)}) collective-permute-start(s16[400,256]{1,0:T(8,128)(2,1)S(1)} %collective-permute-done.17.rest_3_), channel_id=1, source_target_pairs={{0,64},{64,128},{128,192},{192,0},{1,65},{65,129},{129,193},{193,1... | collective-permute-start | bytes 614408 | tf_op jit(solution)/shard_map/ppermute | solution.py:735
where the time goes:
time: 240 us
  waiting for transfers between devices  132 us (55%)
  starting transfers between devices  55.5 us (23%)
  Pallas kernels  50.6 us (21%)
    all_to_all x1, waiting for transfers between devices, per_device(): lax.all_to_all(outgoing, 'block', split_axis=0, concat_axis=0, tiled=True)  66 us
    ppermute x15, waiting for transfers between devices, around(): lax.ppermute(x, 'view', [(i, (i + shift) % VIEWS) for i in range(VIEWS)])  48.2 us
    ppermute x15, starting transfers between devices, around(): lax.ppermute(x, 'view', [(i, (i + shift) % VIEWS) for i in range(VIEWS)])  31.5 us
    ppermute x4, waiting for transfers between devices, swapped(): return lax.ppermute(x, 'block', pairs) if pairs else jnp.zeros_like(x)  17.5 us
    pallas_call x1, Pallas kernels, second(): pl.pallas_call(functools.partial(second_body, layout), out_shape=(cell_sh...  10.6 us
    all_to_all x1, starting transfers between devices, per_device(): lax.all_to_all(outgoing, 'block', split_axis=0, concat_axis=0, tiled=True)  10 us
    pallas_call x1, Pallas kernels, unpack(): pl.pallas_call(functools.partial(unpack_body, cap, chunk), grid=(groups /...  7.91 us
    pallas_call x3, Pallas kernels, mirror(): pl.pallas_call(functools.partial(mirror_body, views, layout, first, last)...  7.85 us
  transfers between devices with their start and end apart: 22, of which 8 were waited for; matrix products, arithmetic and copies ran while one was open for 0% of the time, Pallas kernels for 12%

commit v1 on v0

--- a/solution.py
+++ b/solution.py
@@ -263,6 +263,36 @@
     )(blocks, columns, pltpu.with_memory_space_constraint(tiles, pltpu.HBM))
 
 
+def tucked(code):
+    n = code.shape[0]
+    ends = from_code(code[:, YQ:])
+    turned = [pltpu.roll(ends[j * n // 4 : (j + 1) * n // 4], 48, 1) for j in range(4)]
+    lane = lax.broadcasted_iota(i32, turned[0].shape, 1)
+    rows = [
+        jnp.where(lane < 96, turned[i], pltpu.roll(turned[3], 96 - 32 * i, 1)) for i in range(3)
+    ]
+    rows = jnp.concatenate(rows, axis=0)
+    half = 3 * n // 8
+    rows = jnp.concatenate([rows[:half], rows[half:]], axis=1)
+    return jnp.concatenate([code[:, :YQ], to_code(rows)], axis=0)
+
+
+def untucked(part):
+    if part.shape[1] == YE:
+        return part[...]
+    n = part.shape[0] * 8 // 11
+    rows = from_code(part[n:])
+    rows = jnp.concatenate([rows[:, :128], rows[:, 128:]], axis=0)
+    rows = [rows[i * n // 4 : (i + 1) * n // 4] for i in range(3)]
+    lane = lax.broadcasted_iota(i32, rows[0].shape, 1)
+    last = pltpu.roll(rows[0], 32, 1)
+    for i in (1, 2):
+        moved = pltpu.roll(rows[i], 32 + 32 * i, 1)
+        last = jnp.where((lane >= 32 * i) & (lane < 32 * i + 32), moved, last)
+    ends = [pltpu.roll(row, 80, 1) for row in rows + [last]]
+    return jnp.concatenate([part[:n], to_code(jnp.concatenate(ends, axis=0))], axis=1)
+
+
 PART_VIEWS = (0, 1, 2, 2, 3)
 PART_ROWS = (0, 0, 0, ROWS // 2, 0)
 
@@ -341,13 +371,16 @@
 
         lax.fori_loop(0, BX // 2, pair, 0, unroll=2)
         for r, at, out in zip(PART_VIEWS, PART_ROWS, outs):
-            out[...] = codes[lax.rem(layer + r, VIEWS), at : at + out.shape[0], :]
+            n = out.shape[0] * 8 // 11 if r else out.shape[0]
+            code = codes[lax.rem(layer + r, VIEWS), at : at + n, :]
+            out[...] = tucked(code) if r else code
 
 
 def unpack(cap, place, arrived):
     groups = arrived.shape[0]
     chunk = min(32, groups)
-    shapes = [(ROWS // PART_VIEWS.count(r), YE) for r in PART_VIEWS]
+    rows = [ROWS // PART_VIEWS.count(r) for r in PART_VIEWS]
+    shapes = [(n * 11 // 8, YQ) if r else (n, YE) for n, r in zip(rows, PART_VIEWS)]
     smem = pl.BlockSpec(memory_space=pltpu.SMEM)
     return pl.pallas_call(
         functools.partial(unpack_body, cap, chunk),
@@ -540,7 +573,7 @@
 
 
 def joined(parts):
-    return jnp.concatenate([part[...] for part in parts], axis=0)
+    return jnp.concatenate([untucked(part) for part in parts], axis=0)
 
 
 def grouped(refs, layout):

time: 240 us -> 237 us (0.988)
  the two profiles are of different devices: /device:TPU:11 before, /device:TPU:58 now
where the time goes in v1:
time: 237 us; the launch traced here: 235 us
  waiting for transfers between devices  128 us (54%)
  starting transfers between devices  54.4 us (23%)
  Pallas kernels  51.4 us (22%)
    all_to_all x1, waiting for transfers between devices, per_device(): lax.all_to_all(outgoing, 'block', split_axis=0, concat_axis=0, tiled=True)  70.5 us
    ppermute x15, waiting for transfers between devices, around(): lax.ppermute(x, 'view', [(i, (i + shift) % VIEWS) for i in range(VIEWS)])  41.7 us
    ppermute x15, starting transfers between devices, around(): lax.ppermute(x, 'view', [(i, (i + shift) % VIEWS) for i in range(VIEWS)])  33.6 us
    ppermute x4, waiting for transfers between devices, swapped(): return lax.ppermute(x, 'block', pairs) if pairs else jnp.zeros_like(x)  15.4 us
    pallas_call x1, Pallas kernels, second(): pl.pallas_call(functools.partial(second_body, layout), out_shape=(cell_sh...  10.5 us
    all_to_all x1, starting transfers between devices, per_device(): lax.all_to_all(outgoing, 'block', split_axis=0, concat_axis=0, tiled=True)  9.28 us
    pallas_call x1, Pallas kernels, unpack(): pl.pallas_call(functools.partial(unpack_body, cap, chunk), grid=(groups /...  8.55 us
    pallas_call x3, Pallas kernels, mirror(): pl.pallas_call(functools.partial(mirror_body, views, layout, first, last)...  8.04 us
  transfers between devices with their start and end apart: 22, of which 11 were waited for; matrix products, arithmetic and copies ran while one was open for 0% of the time, Pallas kernels for 13%

profile of v1, /device:TPU:58, one launch (start us, length us, event | category | flops | bytes accessed | tf_op | source)
XLA Modules:
  0.0 235.5 jit_solution(1246172433689909925)
XLA Ops:
  0.0 5.8 %shard_map.55 = bf16[64,400,128]{2,1,0:T(8,128)(2,1)} custom-call(s32[80]{0:T(128)} %bitcast.11, s32[80]{0:T(128)} %bitcast.12, bf16[80,24,1024]{2,1,0:T(8,128)(2,1)} %bitcast.8), custom_call_target="tpu_custom_call" | custom-call | bytes 7864320 | tf_op jit(solution)/shard_map/pallas_call | solution.py:247
  5.8 0.0 copy-start.5
  5.8 0.0 copy-start
  5.9 9.3 %all-to-all-start = ((bf16[64,400,128]{2,1,0:T(8,128)(2,1)}), bf16[64,400,128]{2,1,0:T(8,128)(2,1)}, u32[]{:S(2)}, u32[]{:S(2)}) async-start(bf16[64,400,128]{2,1,0:T(8,128)(2,1)} %shard_map.55), calls=%async_computation | async-start | bytes 13107200 | tf_op jit(solution)/shard_map/all_to_all | solution.py:781
  15.2 0.1 reduce_sum.9
  15.3 0.1 fusion
  15.4 5.4 %collective-permute-start.2 = (f32[3,31]{1,0:T(4,128)S(1)}, f32[3,31]{1,0:T(4,128)S(1)}, u32[]{:S(2)}, u32[]{:S(2)}) collective-permute-start(f32[3,31]{1,0:T(4,128)S(1)} %fusion), channel_id=1, source_target_pairs={{0,192},{64,0},{128,64},{192,128},{1,193},{65,1},{129,65},{193,129... | collective-permute-start | bytes 1124 | tf_op jit(solution)/shard_map/ppermute | solution.py:768
  20.8 1.4 collective-permute-start.1
  22.2 2.4 %collective-permute-start = (f32[3,31]{1,0:T(4,128)S(1)}, f32[3,31]{1,0:T(4,128)S(1)}, u32[]{:S(2)}, u32[]{:S(2)}) collective-permute-start(f32[3,31]{1,0:T(4,128)S(1)} %fusion), channel_id=1, source_target_pairs={{0,64},{64,128},{128,192},{192,0},{1,65},{65,129},{129,193},{193,1... | collective-permute-start | bytes 1124 | tf_op jit(solution)/shard_map/ppermute | solution.py:768
  24.6 0.1 pad_add_fusion.place
  24.7 2.1 shard_map.56
  26.7 1.0 copy-done.1
  27.7 1.9 collective-permute-start.3
  29.7 3.6 %collective-permute-start.4 = (s16[3,128,384]{2,1,0:T(8,128)(2,1)}, s16[3,128,384]{2,1,0:T(8,128)(2,1)S(1)}, u32[]{:S(2)}, u32[]{:S(2)}) collective-permute-start(s16[3,128,384]{2,1,0:T(8,128)(2,1)} %get-tuple-element.50), channel_id=1, source_target_pairs={{1,0},{2,1},{3,2},{4,3},{5,4},{6,5},{7,6},{8,7},{9,8},{10,9},{11,1... | collective-permute-start | bytes 884744 | tf_op jit(solution)/shard_map/ppermute | solution.py:772
  33.3 70.5 %all-to-all-done.arrived.whole_arrived = bf16[64,400,128]{2,1,0:T(8,128)(2,1)} async-done(((bf16[64,400,128]{2,1,0:T(8,128)(2,1)}), bf16[64,400,128]{2,1,0:T(8,128)(2,1)}, u32[]{:S(2)}, u32[]{:S(2)}) %all-to-all-start) | async-done | bytes 6553632 | tf_op jit(solution)/shard_map/all_to_all | solution.py:781
  103.8 8.6 %shard_map.57 = (s16[768,384]{1,0:T(8,128)(2,1)S(1)}, s16[1056,256]{1,0:T(8,128)(2,1)S(1)}, s16[528,256]{1,0:T(8,128)(2,1)S(1)}, s16[528,256]{1,0:T(8,128)(2,1)S(1)}, s16[1056,256]{1,0:T(8,128)(2,1)S(1)}) custom-call(s32[2]{0:T(128)S(1)} %pad_add_fusion.place, bf16[64,400,128]{2,1,0:T(8,128)(2,1)} %all-to-all-done.arrived.whole_arrived, ...), custom_call_target="tpu_custom_call" | custom-call | flops 3276800 | bytes 6553600 | tf_op jit(solution)/shard_map/pallas_call | solution.py:385
  112.4 0.0 collective-permute-done.2
  112.4 0.0 collective-permute-done
  112.4 0.1 stack.27
  112.5 0.1 stack.28
  112.5 0.1 stack.29
  112.6 0.1 stack.30
  112.7 3.0 %collective-permute-start.7 = (s16[528,256]{1,0:T(8,128)(2,1)S(1)}, s16[528,256]{1,0:T(8,128)(2,1)S(1)}, u32[]{:S(2)}, u32[]{:S(2)}) collective-permute-start(s16[528,256]{1,0:T(8,128)(2,1)S(1)} %get-tuple-element.64), channel_id=1, source_target_pairs={{0,64},{64,128},{128,192},{192,0},{1,65},{65,129},{129,193},{193,1... | collective-permute-start | bytes 811016 | tf_op jit(solution)/shard_map/ppermute | solution.py:768
  115.7 1.8 collective-permute-start.9
  117.6 1.7 collective-permute-start.5
  119.3 0.0 copy-start.2
  119.3 5.3 %shard_map.58 = (bf16[4,256,512]{2,1,0:T(8,128)(2,1)S(1)}, bf16[4,512,256]{2,1,0:T(8,128)(2,1)S(1)}, bf16[4,384,384]{2,1,0:T(8,128)(2,1)S(1)}, bf16[4,384,384]{2...) custom-call(f32[4,93]{1,0:T(4,128)S(1)} %pad_maximum_fusion.taps), custom_call_target="tpu_custom_call" | custom-call | flops 4000000000 | bytes 20000000 | tf_op jit(solution)/shard_map/pallas_call | solution.py:453
  124.6 2.6 %collective-permute-start.6 = (s16[1056,256]{1,0:T(8,128)(2,1)S(1)}, s16[1056,256]{1,0:T(8,128)(2,1)S(1)}, u32[]{:S(2)}, u32[]{:S(2)}) collective-permute-start(s16[1056,256]{1,0:T(8,128)(2,1)S(1)} %get-tuple-element.63), channel_id=1, source_target_pairs={{0,192},{64,0},{128,64},{192,128},{1,193},{65,1},{129,65},{193,129... | collective-permute-start | bytes 1622024 | tf_op jit(solution)/shard_map/ppermute | solution.py:768
  127.3 5.5 %shard_map.59.rest_1_.rest_3_ = f32[4,768,384]{2,1,0:T(8,128)S(1)} custom-call(f32[3,256,384]{2,1,0:T(8,128)S(1)} %copy-done.2, s16[3,128,384]{2,1,0:T(8,128)(2,1)S(1)} %collective-permute-done.3.from_left.e_left, s16[3,128,384]{2,1,0:T(8,128)(2,1)S(1)} %collective-permute-done.4.from_right.e_right, bf16[4,256,512]{2,1,0:T(8,128)(2,1)S(1)} %get-tuple-element.56.kx.rest_5_, ...), custom_call_target="tpu_custom_call" | custom-call | flops 7000000000 | bytes 16000000 | tf_op jit(solution)/shard_map/pallas_call | solution.py:563
  132.8 2.0 shard_map.60.rest_0_
  134.8 1.4 collective-permute-done.7
  136.2 0.5 collective-permute-start.8
  136.7 0.0 collective-permute-done.9
  136.7 3.6 %collective-permute-start.10 = (s16[528,256]{1,0:T(8,128)(2,1)S(1)}, s16[528,256]{1,0:T(8,128)(2,1)S(1)}, u32[]{:S(2)}, u32[]{:S(2)}) collective-permute-start(s16[528,256]{1,0:T(8,128)(2,1)S(1)} %collective-permute-done.9), channel_id=1, source_target_pairs={{0,192},{64,0},{128,64},{192,128},{1,193},{65,1},{129,65},{193,129... | collective-permute-start | bytes 811016 | tf_op jit(solution)/shard_map/ppermute | solution.py:768
  140.3 7.4 %collective-permute-done.5.rest_1_ = s16[1056,256]{1,0:T(8,128)(2,1)S(1)} collective-permute-done((s16[1056,256]{1,0:T(8,128)(2,1)S(1)}, s16[1056,256]{1,0:T(8,128)(2,1)S(1)}, u32[]{:S(2)}, u32[]{:S(2)}) %collective-permute-start.5) | collective-permute-done | bytes 540704 | tf_op jit(solution)/shard_map/ppermute | solution.py:768
  147.8 0.0 collective-permute-done.6.rest_2_.rest_4_
  147.8 3.4 %shard_map.61.rest_0_ = f32[3,512,384]{2,1,0:T(8,128)S(1)} custom-call(s32[2]{0:T(128)S(1)} %pad_add_fusion.place, f32[3,512,384]{2,1,0:T(8,128)S(1)} %shard_map.60.rest_0_, s16[1056,256]{1,0:T(8,128)(2,1)S(1)} %collective-permute-done.5.rest_1_, s16[1056,256]{1,0:T(8,128)(2,1)S(1)} %collective-permute-done.6.rest_2_.rest_4_, ...), custom_call_target="tpu_custom_call" | custom-call | flops 4000000000 | bytes 16000000 | tf_op jit(solution)/shard_map/pallas_call | solution.py:606
  151.2 2.3 collective-permute-done.8.rest_1_.rest_2_
  153.4 9.5 %collective-permute-done.10.rest_2_.rest_3_ = s16[528,256]{1,0:T(8,128)(2,1)S(1)} collective-permute-done((s16[528,256]{1,0:T(8,128)(2,1)S(1)}, s16[528,256]{1,0:T(8,128)(2,1)S(1)}, u32[]{:S(2)}, u32[]{:S(2)}) %collective-permute-start.10) | collective-permute-done | bytes 270368 | tf_op jit(solution)/shard_map/ppermute | solution.py:768
  162.9 2.7 %shard_map.62 = (f32[3,512,384]{2,1,0:T(8,128)S(1)}, s16[992,256]{1,0:T(8,128)(2,1)S(1)}, s16[992,256]{1,0:T(8,128)(2,1)S(1)}) custom-call(s32[2]{0:T(128)S(1)} %pad_add_fusion.place, f32[3,512,384]{2,1,0:T(8,128)S(1)} %shard_map.61.rest_0_, s16[528,256]{1,0:T(8,128)(2,1)S(1)} %collective-permute-done.8.rest_1_.rest_2_, ...), custom_call_target="tpu_custom_call" | custom-call | flops 2000000000 | bytes 8000000 | tf_op jit(solution)/shard_map/pallas_call | solution.py:606
  165.7 1.9 collective-permute-start.11
  167.6 0.1 collective-permute-start.12
  167.7 11.4 %collective-permute-done.11.x_first = s16[992,256]{1,0:T(8,128)(2,1)S(1)} collective-permute-done((s16[992,256]{1,0:T(8,128)(2,1)S(1)}, s16[992,256]{1,0:T(8,128)(2,1)S(1)}, u32[]{:S(2)}, u32[]{:S(2)}) %collective-permute-start.11) | collective-permute-done | bytes 507936 | tf_op jit(solution)/shard_map/ppermute | solution.py:778
  179.1 0.0 collective-permute-done.12.x_second
  179.1 10.5 %shard_map.63 = (f32[3,256,256]{2,1,0:T(8,128)S(1)}, f32[3,256,256]{2,1,0:T(8,128)S(1)}, s16[400,256]{1,0:T(8,128)(2,1)S(1)}, s16[400,256]{1,0:T(8,128)(2,1)S(1)}) custom-call(s32[2]{0:T(128)S(1)} %pad_add_fusion.place, f32[3,256,384]{2,1,0:T(8,128)S(1)} %copy-done.2, s16[3,128,384]{2,1,0:T(8,128)(2,1)S(1)} %collective-permute-done.3.from_left.e_left, ...), custom_call_target="tpu_custom_call" | custom-call | flops 16000000000 | bytes 40000000 | tf_op jit(solution)/shard_map/pallas_call | solution.py:657
  189.6 2.8 %collective-permute-start.13 = (s16[400,256]{1,0:T(8,128)(2,1)S(1)}, s16[400,256]{1,0:T(8,128)(2,1)S(1)}, u32[]{:S(2)}, u32[]{:S(2)}) collective-permute-start(s16[400,256]{1,0:T(8,128)(2,1)S(1)} %get-tuple-element.71), channel_id=1, source_target_pairs={{1,2},{2,1},{3,4},{4,3},{5,6},{6,5},{7,8},{8,7},{9,10},{10,9},{11,... | collective-permute-start | bytes 614408 | tf_op jit(solution)/shard_map/ppermute | solution.py:778
  192.4 1.1 collective-permute-start.14
  193.6 4.0 %collective-permute-done.13.x_first = s16[400,256]{1,0:T(8,128)(2,1)S(1)} collective-permute-done((s16[400,256]{1,0:T(8,128)(2,1)S(1)}, s16[400,256]{1,0:T(8,128)(2,1)S(1)}, u32[]{:S(2)}, u32[]{:S(2)}) %collective-permute-start.13) | collective-permute-done | bytes 204832 | tf_op jit(solution)/shard_map/ppermute | solution.py:778
  197.6 0.0 collective-permute-done.14.x_second
  197.6 1.0 shard_map.64
  198.6 2.5 %collective-permute-start.15 = (s16[400,256]{1,0:T(8,128)(2,1)S(1)}, s16[400,256]{1,0:T(8,128)(2,1)S(1)}, u32[]{:S(2)}, u32[]{:S(2)}) collective-permute-start(s16[400,256]{1,0:T(8,128)(2,1)S(1)} %get-tuple-element.73.rest_0_), channel_id=1, source_target_pairs={{0,192},{64,0},{128,64},{192,128},{1,193},{65,1},{129,65},{193,129... | collective-permute-start | bytes 614408 | tf_op jit(solution)/shard_map/ppermute | solution.py:768
  201.1 0.5 collective-permute-start.17
  201.6 3.5 %collective-permute-start.19 = (s16[400,256]{1,0:T(8,128)(2,1)S(1)}, s16[400,256]{1,0:T(8,128)(2,1)S(1)}, u32[]{:S(2)}, u32[]{:S(2)}) collective-permute-start(s16[400,256]{1,0:T(8,128)(2,1)S(1)} %get-tuple-element.73.rest_0_), channel_id=1, source_target_pairs={{0,64},{64,128},{128,192},{192,0},{1,65},{65,129},{129,193},{193,1... | collective-permute-start | bytes 614408 | tf_op jit(solution)/shard_map/ppermute | solution.py:768
  205.1 0.7 collective-permute-start.20
  205.7 10.2 %collective-permute-done.15.rest_4_ = s16[400,256]{1,0:T(8,128)(2,1)S(1)} collective-permute-done((s16[400,256]{1,0:T(8,128)(2,1)S(1)}, s16[400,256]{1,0:T(8,128)(2,1)S(1)}, u32[]{:S(2)}, u32[]{:S(2)}) %collective-permute-start.15) | collective-permute-done | bytes 204832 | tf_op jit(solution)/shard_map/ppermute | solution.py:768
  215.9 3.7 %collective-permute-start.16 = (s16[400,256]{1,0:T(8,128)(2,1)S(1)}, s16[400,256]{1,0:T(8,128)(2,1)S(1)}, u32[]{:S(2)}, u32[]{:S(2)}) collective-permute-start(s16[400,256]{1,0:T(8,128)(2,1)S(1)} %collective-permute-done.15.rest_4_), channel_id=1, source_target_pairs={{0,192},{64,0},{128,64},{192,128},{1,193},{65,1},{129,65},{193,129... | collective-permute-start | bytes 614408 | tf_op jit(solution)/shard_map/ppermute | solution.py:768
  219.7 3.7 %collective-permute-done.17.rest_3_ = s16[400,256]{1,0:T(8,128)(2,1)S(1)} collective-permute-done((s16[400,256]{1,0:T(8,128)(2,1)S(1)}, s16[400,256]{1,0:T(8,128)(2,1)S(1)}, u32[]{:S(2)}, u32[]{:S(2)}) %collective-permute-start.17) | collective-permute-done | bytes 204832 | tf_op jit(solution)/shard_map/ppermute | solution.py:768
  223.4 0.1 collective-permute-start.18
  223.5 4.3 %collective-permute-done.19.rest_2_ = s16[400,256]{1,0:T(8,128)(2,1)S(1)} collective-permute-done((s16[400,256]{1,0:T(8,128)(2,1)S(1)}, s16[400,256]{1,0:T(8,128)(2,1)S(1)}, u32[]{:S(2)}, u32[]{:S(2)}) %collective-permute-start.19) | collective-permute-done | bytes 204832 | tf_op jit(solution)/shard_map/ppermute | solution.py:768
  227.7 0.0 collective-permute-done.20.rest_5_
  227.7 3.0 %shard_map.65._ = f32[24,32,1024]{2,1,0:T(8,128)} custom-call(s32[2]{0:T(128)S(1)} %pad_add_fusion.place, s16[400,256]{1,0:T(8,128)(2,1)S(1)} %get-tuple-element.73.rest_0_, s16[400,256]{1,0:T(8,128)(2,1)S(1)} %get-tuple-element.74.rest_1_, s16[400,256]{1,0:T(8,128)(2,1)S(1)} %collective-permute-done.19.rest_2_, ...), custom_call_target="tpu_custom_call" | custom-call | flops 3000000 | bytes 6000000 | tf_op jit(solution)/shard_map/pallas_call | solution.py:721
  230.7 0.0 collective-permute-done.16.low
  230.7 2.9 %collective-permute-done.18.high = s16[400,256]{1,0:T(8,128)(2,1)S(1)} collective-permute-done((s16[400,256]{1,0:T(8,128)(2,1)S(1)}, s16[400,256]{1,0:T(8,128)(2,1)S(1)}, u32[]{:S(2)}, u32[]{:S(2)}) %collective-permute-start.18) | collective-permute-done | bytes 204832 | tf_op jit(solution)/shard_map/ppermute | solution.py:768
  233.6 1.7 shard_map.66
  (13 shorter events, 0.0 us)
Async XLA Ops:
  5.8 9.3 %copy-start.5 = (f32[1,3,31]{2,0,1:T(1,128)S(1)}, f32[1,3,31]{2,0,1:T(1,128)}, u32[]{:S(2)}) copy-start(f32[1,3,31]{2,0,1:T(1,128)} %param.8) | copy-start | bytes 1120
  5.8 18.8 %copy-start = (f32[24,32,1024]{2,1,0:T(8,128)S(1)}, f32[24,32,1024]{2,1,0:T(8,128)}, u32[]{:S(2)}) copy-start(f32[24,32,1024]{2,1,0:T(8,128)} %start) | copy-start | bytes 9437188
  5.9 97.9 %all-to-all-start = ((bf16[64,400,128]{2,1,0:T(8,128)(2,1)}), bf16[64,400,128]{2,1,0:T(8,128)(2,1)}, u32[]{:S(2)}, u32[]{:S(2)}) async-start(bf16[64,400,128]{2,1,0:T(8,128)(2,1)} %shard_map.55), calls=%async_computation | async-start | bytes 13107200 | tf_op jit(solution)/shard_map/all_to_all | solution.py:781
  15.4 97.0 %collective-permute-start.2 = (f32[3,31]{1,0:T(4,128)S(1)}, f32[3,31]{1,0:T(4,128)S(1)}, u32[]{:S(2)}, u32[]{:S(2)}) collective-permute-start(f32[3,31]{1,0:T(4,128)S(1)} %fusion), channel_id=1, source_target_pairs={{0,192},{64,0},{128,64},{192,128},{1,193},{65,1},{129,65},{193,129... | collective-permute-start | bytes 1124 | tf_op jit(solution)/shard_map/ppermute | solution.py:768
  20.8 91.6 %collective-permute-start.1 = (f32[3,31]{1,0:T(4,128)S(1)}, f32[3,31]{1,0:T(4,128)S(1)}, u32[]{:S(2)}, u32[]{:S(2)}) collective-permute-start(f32[3,31]{1,0:T(4,128)S(1)} %fusion), channel_id=1, source_target_pairs={{0,128},{64,192},{128,0},{192,64},{1,129},{65,193},{129,1},{193,65... | collective-permute-start | bytes 1124 | tf_op jit(solution)/shard_map/ppermute | solution.py:768
  22.2 90.2 %collective-permute-start = (f32[3,31]{1,0:T(4,128)S(1)}, f32[3,31]{1,0:T(4,128)S(1)}, u32[]{:S(2)}, u32[]{:S(2)}) collective-permute-start(f32[3,31]{1,0:T(4,128)S(1)} %fusion), channel_id=1, source_target_pairs={{0,64},{64,128},{128,192},{192,0},{1,65},{65,129},{129,193},{193,1... | collective-permute-start | bytes 1124 | tf_op jit(solution)/shard_map/ppermute | solution.py:768
  26.7 1.0 copy-start.1
  27.7 96.9 %collective-permute-start.3 = (s16[3,128,384]{2,1,0:T(8,128)(2,1)}, s16[3,128,384]{2,1,0:T(8,128)(2,1)S(1)}, u32[]{:S(2)}, u32[]{:S(2)}) collective-permute-start(s16[3,128,384]{2,1,0:T(8,128)(2,1)} %get-tuple-element.49), channel_id=1, source_target_pairs={{0,1},{1,2},{2,3},{3,4},{4,5},{5,6},{6,7},{7,8},{8,9},{9,10},{10,1... | collective-permute-start | bytes 884744 | tf_op jit(solution)/shard_map/ppermute | solution.py:772
  29.7 97.6 %collective-permute-start.4 = (s16[3,128,384]{2,1,0:T(8,128)(2,1)}, s16[3,128,384]{2,1,0:T(8,128)(2,1)S(1)}, u32[]{:S(2)}, u32[]{:S(2)}) collective-permute-start(s16[3,128,384]{2,1,0:T(8,128)(2,1)} %get-tuple-element.50), channel_id=1, source_target_pairs={{1,0},{2,1},{3,2},{4,3},{5,4},{6,5},{7,6},{8,7},{9,8},{10,9},{11,1... | collective-permute-start | bytes 884744 | tf_op jit(solution)/shard_map/ppermute | solution.py:772
  112.7 23.5 %collective-permute-start.7 = (s16[528,256]{1,0:T(8,128)(2,1)S(1)}, s16[528,256]{1,0:T(8,128)(2,1)S(1)}, u32[]{:S(2)}, u32[]{:S(2)}) collective-permute-start(s16[528,256]{1,0:T(8,128)(2,1)S(1)} %get-tuple-element.64), channel_id=1, source_target_pairs={{0,64},{64,128},{128,192},{192,0},{1,65},{65,129},{129,193},{193,1... | collective-permute-start | bytes 811016 | tf_op jit(solution)/shard_map/ppermute | solution.py:768
  115.7 21.0 %collective-permute-start.9 = (s16[528,256]{1,0:T(8,128)(2,1)S(1)}, s16[528,256]{1,0:T(8,128)(2,1)S(1)}, u32[]{:S(2)}, u32[]{:S(2)}) collective-permute-start(s16[528,256]{1,0:T(8,128)(2,1)S(1)} %get-tuple-element.65), channel_id=1, source_target_pairs={{0,192},{64,0},{128,64},{192,128},{1,193},{65,1},{129,65},{193,129... | collective-permute-start | bytes 811016 | tf_op jit(solution)/shard_map/ppermute | solution.py:768
  117.6 30.2 %collective-permute-start.5 = (s16[1056,256]{1,0:T(8,128)(2,1)S(1)}, s16[1056,256]{1,0:T(8,128)(2,1)S(1)}, u32[]{:S(2)}, u32[]{:S(2)}) collective-permute-start(s16[1056,256]{1,0:T(8,128)(2,1)S(1)} %get-tuple-element.62), channel_id=1, source_target_pairs={{0,64},{64,128},{128,192},{192,0},{1,65},{65,129},{129,193},{193,1... | collective-permute-start | bytes 1622024 | tf_op jit(solution)/shard_map/ppermute | solution.py:768
  119.3 7.9 %copy-start.2 = (f32[3,256,384]{2,1,0:T(8,128)S(1)}, f32[3,256,384]{2,1,0:T(8,128)}, u32[]{:S(2)}) copy-start(f32[3,256,384]{2,1,0:T(8,128)} %copy-done.1) | copy-start | bytes 3538948
  124.6 23.2 %collective-permute-start.6 = (s16[1056,256]{1,0:T(8,128)(2,1)S(1)}, s16[1056,256]{1,0:T(8,128)(2,1)S(1)}, u32[]{:S(2)}, u32[]{:S(2)}) collective-permute-start(s16[1056,256]{1,0:T(8,128)(2,1)S(1)} %get-tuple-element.63), channel_id=1, source_target_pairs={{0,192},{64,0},{128,64},{192,128},{1,193},{65,1},{129,65},{193,129... | collective-permute-start | bytes 1622024 | tf_op jit(solution)/shard_map/ppermute | solution.py:768
  127.3 5.5 %copy-start.3 = (s16[3,128,384]{2,1,0:T(8,128)(2,1)}, s16[3,128,384]{2,1,0:T(8,128)(2,1)S(1)}, u32[]{:S(2)}) copy-start(s16[3,128,384]{2,1,0:T(8,128)(2,1)S(1)} %collective-permute-done.4.from_right.e_right) | copy-start | bytes 884740
  136.2 17.2 %collective-permute-start.8 = (s16[528,256]{1,0:T(8,128)(2,1)S(1)}, s16[528,256]{1,0:T(8,128)(2,1)S(1)}, u32[]{:S(2)}, u32[]{:S(2)}) collective-permute-start(s16[528,256]{1,0:T(8,128)(2,1)S(1)} %collective-permute-done.7), channel_id=1, source_target_pairs={{0,64},{64,128},{128,192},{192,0},{1,65},{65,129},{129,193},{193,1... | collective-permute-start | bytes 811016 | tf_op jit(solution)/shard_map/ppermute | solution.py:768
  136.7 26.2 %collective-permute-start.10 = (s16[528,256]{1,0:T(8,128)(2,1)S(1)}, s16[528,256]{1,0:T(8,128)(2,1)S(1)}, u32[]{:S(2)}, u32[]{:S(2)}) collective-permute-start(s16[528,256]{1,0:T(8,128)(2,1)S(1)} %collective-permute-done.9), channel_id=1, source_target_pairs={{0,192},{64,0},{128,64},{192,128},{1,193},{65,1},{129,65},{193,129... | collective-permute-start | bytes 811016 | tf_op jit(solution)/shard_map/ppermute | solution.py:768
  151.1 28.0 %copy-start.4 = (s16[3,128,384]{2,1,0:T(8,128)(2,1)S(1)}, s16[3,128,384]{2,1,0:T(8,128)(2,1)}, u32[]{:S(2)}) copy-start(s16[3,128,384]{2,1,0:T(8,128)(2,1)} %copy-done.3) | copy-start | bytes 884740
  165.7 13.4 %collective-permute-start.11 = (s16[992,256]{1,0:T(8,128)(2,1)S(1)}, s16[992,256]{1,0:T(8,128)(2,1)S(1)}, u32[]{:S(2)}, u32[]{:S(2)}) collective-permute-start(s16[992,256]{1,0:T(8,128)(2,1)S(1)} %get-tuple-element.67), channel_id=1, source_target_pairs={{1,2},{2,1},{3,4},{4,3},{5,6},{6,5},{7,8},{8,7},{9,10},{10,9},{11,... | collective-permute-start | bytes 1523720 | tf_op jit(solution)/shard_map/ppermute | solution.py:778
  167.6 11.5 %collective-permute-start.12 = (s16[992,256]{1,0:T(8,128)(2,1)S(1)}, s16[992,256]{1,0:T(8,128)(2,1)S(1)}, u32[]{:S(2)}, u32[]{:S(2)}) collective-permute-start(s16[992,256]{1,0:T(8,128)(2,1)S(1)} %get-tuple-element.68), channel_id=1, source_target_pairs={{0,1},{1,0},{2,3},{3,2},{4,5},{5,4},{6,7},{7,6},{8,9},{9,8},{10,11... | collective-permute-start | bytes 1523720 | tf_op jit(solution)/shard_map/ppermute | solution.py:778
  189.6 8.0 %collective-permute-start.13 = (s16[400,256]{1,0:T(8,128)(2,1)S(1)}, s16[400,256]{1,0:T(8,128)(2,1)S(1)}, u32[]{:S(2)}, u32[]{:S(2)}) collective-permute-start(s16[400,256]{1,0:T(8,128)(2,1)S(1)} %get-tuple-element.71), channel_id=1, source_target_pairs={{1,2},{2,1},{3,4},{4,3},{5,6},{6,5},{7,8},{8,7},{9,10},{10,9},{11,... | collective-permute-start | bytes 614408 | tf_op jit(solution)/shard_map/ppermute | solution.py:778
  192.4 5.2 %collective-permute-start.14 = (s16[400,256]{1,0:T(8,128)(2,1)S(1)}, s16[400,256]{1,0:T(8,128)(2,1)S(1)}, u32[]{:S(2)}, u32[]{:S(2)}) collective-permute-start(s16[400,256]{1,0:T(8,128)(2,1)S(1)} %get-tuple-element.72), channel_id=1, source_target_pairs={{0,1},{1,0},{2,3},{3,2},{4,5},{5,4},{6,7},{7,6},{8,9},{9,8},{10,11... | collective-permute-start | bytes 614408 | tf_op jit(solution)/shard_map/ppermute | solution.py:778
  198.6 17.3 %collective-permute-start.15 = (s16[400,256]{1,0:T(8,128)(2,1)S(1)}, s16[400,256]{1,0:T(8,128)(2,1)S(1)}, u32[]{:S(2)}, u32[]{:S(2)}) collective-permute-start(s16[400,256]{1,0:T(8,128)(2,1)S(1)} %get-tuple-element.73.rest_0_), channel_id=1, source_target_pairs={{0,192},{64,0},{128,64},{192,128},{1,193},{65,1},{129,65},{193,129... | collective-permute-start | bytes 614408 | tf_op jit(solution)/shard_map/ppermute | solution.py:768
  201.1 22.2 %collective-permute-start.17 = (s16[400,256]{1,0:T(8,128)(2,1)S(1)}, s16[400,256]{1,0:T(8,128)(2,1)S(1)}, u32[]{:S(2)}, u32[]{:S(2)}) collective-permute-start(s16[400,256]{1,0:T(8,128)(2,1)S(1)} %get-tuple-element.74.rest_1_), channel_id=1, source_target_pairs={{0,64},{64,128},{128,192},{192,0},{1,65},{65,129},{129,193},{193,1... | collective-permute-start | bytes 614408 | tf_op jit(solution)/shard_map/ppermute | solution.py:768
  201.6 26.1 %collective-permute-start.19 = (s16[400,256]{1,0:T(8,128)(2,1)S(1)}, s16[400,256]{1,0:T(8,128)(2,1)S(1)}, u32[]{:S(2)}, u32[]{:S(2)}) collective-permute-start(s16[400,256]{1,0:T(8,128)(2,1)S(1)} %get-tuple-element.73.rest_0_), channel_id=1, source_target_pairs={{0,64},{64,128},{128,192},{192,0},{1,65},{65,129},{129,193},{193,1... | collective-permute-start | bytes 614408 | tf_op jit(solution)/shard_map/ppermute | solution.py:768
  205.1 22.7 %collective-permute-start.20 = (s16[400,256]{1,0:T(8,128)(2,1)S(1)}, s16[400,256]{1,0:T(8,128)(2,1)S(1)}, u32[]{:S(2)}, u32[]{:S(2)}) collective-permute-start(s16[400,256]{1,0:T(8,128)(2,1)S(1)} %get-tuple-element.74.rest_1_), channel_id=1, source_target_pairs={{0,192},{64,0},{128,64},{192,128},{1,193},{65,1},{129,65},{193,129... | collective-permute-start | bytes 614408 | tf_op jit(solution)/shard_map/ppermute | solution.py:768
  215.9 14.8 %collective-permute-start.16 = (s16[400,256]{1,0:T(8,128)(2,1)S(1)}, s16[400,256]{1,0:T(8,128)(2,1)S(1)}, u32[]{:S(2)}, u32[]{:S(2)}) collective-permute-start(s16[400,256]{1,0:T(8,128)(2,1)S(1)} %collective-permute-done.15.rest_4_), channel_id=1, source_target_pairs={{0,192},{64,0},{128,64},{192,128},{1,193},{65,1},{129,65},{193,129... | collective-permute-start | bytes 614408 | tf_op jit(solution)/shard_map/ppermute | solution.py:768
  223.4 10.2 %collective-permute-start.18 = (s16[400,256]{1,0:T(8,128)(2,1)S(1)}, s16[400,256]{1,0:T(8,128)(2,1)S(1)}, u32[]{:S(2)}, u32[]{:S(2)}) collective-permute-start(s16[400,256]{1,0:T(8,128)(2,1)S(1)} %collective-permute-done.17.rest_3_), channel_id=1, source_target_pairs={{0,64},{64,128},{128,192},{192,0},{1,65},{65,129},{129,193},{193,1... | collective-permute-start | bytes 614408 | tf_op jit(solution)/shard_map/ppermute | solution.py:768

commit v2 on v1

--- a/solution.py
+++ b/solution.py
@@ -190,7 +190,7 @@
         slots[p] = slot
         return 0
 
-    lax.fori_loop(0, pieces, route, 0)
+    lax.fori_loop(0, pieces, route, 0, unroll=2)
     lane = lax.broadcasted_iota(i32, (16, 128), 1)
 
     def mark(b, _):
@@ -200,7 +200,7 @@
         sent[b, cap * SLOT :, :] = row.astype(f32).astype(bf16)
         return 0
 
-    lax.fori_loop(0, groups, mark, 0)
+    lax.fori_loop(0, groups, mark, 0, unroll=2)
     def push(b, at, rows, sem):
         part = pl.ds(pl.multiple_of(at, 16), rows)
         return pltpu.make_async_copy(sent.at[b, part, :], out.at[b, part, :], sem)
@@ -343,7 +343,7 @@
 
         return 0
 
-    lax.fori_loop(0, chunk, from_source, 0, unroll=4)
+    lax.fori_loop(0, chunk, from_source, 0, unroll=8)
 
     @pl.when(step == pl.num_programs(0) - 1)
     def _():
@@ -369,7 +369,7 @@
                     codes[v, to, :] = to_code(code)
             return 0
 
-        lax.fori_loop(0, BX // 2, pair, 0, unroll=2)
+        lax.fori_loop(0, BX // 2, pair, 0, unroll=4)
         for r, at, out in zip(PART_VIEWS, PART_ROWS, outs):
             n = out.shape[0] * 8 // 11 if r else out.shape[0]
             code = codes[lax.rem(layer + r, VIEWS), at : at + n, :]

time: 237 us -> 237 us (level)
  starting transfers between devices: 54.4 us -> 50.2 us
  waiting for transfers between devices: 128 us -> 131 us
    ppermute x4, waiting for transfers between devices: 15.4 us -> 19.2 us  [swapped(): return lax.ppermute(x, 'block', pairs) if pairs else jnp.zeros_like(x)]
  transfers between devices with their start and end apart: 22 -> 22, of which waited for: 11 -> 12; matrix products, arithmetic and copies ran while one was open for 0% -> 0% of each run, Pallas kernels for 13% -> 13%
where the time goes in v2:
time: 237 us; the launch traced here: 234 us
  waiting for transfers between devices  131 us (55%)
  Pallas kernels  50.5 us (21%)
  starting transfers between devices  50.2 us (21%)
    all_to_all x1, waiting for transfers between devices, per_device(): lax.all_to_all(outgoing, 'block', split_axis=0, concat_axis=0, tiled=True)  70.5 us
    ppermute x15, waiting for transfers between devices, around(): lax.ppermute(x, 'view', [(i, (i + shift) % VIEWS) for i in range(VIEWS)])  41.1 us
    ppermute x15, starting transfers between devices, around(): lax.ppermute(x, 'view', [(i, (i + shift) % VIEWS) for i in range(VIEWS)])  31.3 us
    ppermute x4, waiting for transfers between devices, swapped(): return lax.ppermute(x, 'block', pairs) if pairs else jnp.zeros_like(x)  19.2 us
    pallas_call x1, Pallas kernels, second(): pl.pallas_call(functools.partial(second_body, layout), out_shape=(cell_sh...  10.5 us
    all_to_all x1, starting transfers between devices, per_device(): lax.all_to_all(outgoing, 'block', split_axis=0, concat_axis=0, tiled=True)  9.26 us
    pallas_call x1, Pallas kernels, unpack(): pl.pallas_call(functools.partial(unpack_body, cap, chunk), grid=(groups /...  8.1 us
    pallas_call x3, Pallas kernels, mirror(): pl.pallas_call(functools.partial(mirror_body, views, layout, first, last)...  8.04 us
  transfers between devices with their start and end apart: 22, of which 12 were waited for; matrix products, arithmetic and copies ran while one was open for 0% of the time, Pallas kernels for 13%

profile of v2, /device:TPU:58, one launch (start us, length us, event | category | flops | bytes accessed | tf_op | source)
XLA Modules:
  0.0 233.5 jit_solution(15825550752140708800)
XLA Ops:
  0.0 5.5 %shard_map.55 = bf16[64,400,128]{2,1,0:T(8,128)(2,1)} custom-call(s32[80]{0:T(128)} %bitcast.11, s32[80]{0:T(128)} %bitcast.12, bf16[80,24,1024]{2,1,0:T(8,128)(2,1)} %bitcast.8), custom_call_target="tpu_custom_call" | custom-call | bytes 7864320 | tf_op jit(solution)/shard_map/pallas_call | solution.py:247
  5.5 0.0 copy-start.5
  5.5 0.0 copy-start
  5.5 9.3 %all-to-all-start = ((bf16[64,400,128]{2,1,0:T(8,128)(2,1)}), bf16[64,400,128]{2,1,0:T(8,128)(2,1)}, u32[]{:S(2)}, u32[]{:S(2)}) async-start(bf16[64,400,128]{2,1,0:T(8,128)(2,1)} %shard_map.55), calls=%async_computation | async-start | bytes 13107200 | tf_op jit(solution)/shard_map/all_to_all | solution.py:781
  14.8 0.1 reduce_sum.9
  14.9 0.1 fusion
  15.0 5.4 %collective-permute-start.2 = (f32[3,31]{1,0:T(4,128)S(1)}, f32[3,31]{1,0:T(4,128)S(1)}, u32[]{:S(2)}, u32[]{:S(2)}) collective-permute-start(f32[3,31]{1,0:T(4,128)S(1)} %fusion), channel_id=1, source_target_pairs={{0,192},{64,0},{128,64},{192,128},{1,193},{65,1},{129,65},{193,129... | collective-permute-start | bytes 1124 | tf_op jit(solution)/shard_map/ppermute | solution.py:768
  20.4 1.4 collective-permute-start.1
  21.9 2.4 %collective-permute-start = (f32[3,31]{1,0:T(4,128)S(1)}, f32[3,31]{1,0:T(4,128)S(1)}, u32[]{:S(2)}, u32[]{:S(2)}) collective-permute-start(f32[3,31]{1,0:T(4,128)S(1)} %fusion), channel_id=1, source_target_pairs={{0,64},{64,128},{128,192},{192,0},{1,65},{65,129},{129,193},{193,1... | collective-permute-start | bytes 1124 | tf_op jit(solution)/shard_map/ppermute | solution.py:768
  24.2 0.1 pad_add_fusion.place
  24.3 2.1 shard_map.56
  26.4 1.0 copy-done.1
  27.4 1.9 collective-permute-start.3
  29.3 3.6 %collective-permute-start.4 = (s16[3,128,384]{2,1,0:T(8,128)(2,1)}, s16[3,128,384]{2,1,0:T(8,128)(2,1)S(1)}, u32[]{:S(2)}, u32[]{:S(2)}) collective-permute-start(s16[3,128,384]{2,1,0:T(8,128)(2,1)} %get-tuple-element.50), channel_id=1, source_target_pairs={{1,0},{2,1},{3,2},{4,3},{5,4},{6,5},{7,6},{8,7},{9,8},{10,9},{11,1... | collective-permute-start | bytes 884744 | tf_op jit(solution)/shard_map/ppermute | solution.py:772
  32.9 70.5 %all-to-all-done.arrived.whole_arrived = bf16[64,400,128]{2,1,0:T(8,128)(2,1)} async-done(((bf16[64,400,128]{2,1,0:T(8,128)(2,1)}), bf16[64,400,128]{2,1,0:T(8,128)(2,1)}, u32[]{:S(2)}, u32[]{:S(2)}) %all-to-all-start) | async-done | bytes 6553632 | tf_op jit(solution)/shard_map/all_to_all | solution.py:781
  103.4 8.1 %shard_map.57 = (s16[768,384]{1,0:T(8,128)(2,1)S(1)}, s16[1056,256]{1,0:T(8,128)(2,1)S(1)}, s16[528,256]{1,0:T(8,128)(2,1)S(1)}, s16[528,256]{1,0:T(8,128)(2,1)S(1)}, s16[1056,256]{1,0:T(8,128)(2,1)S(1)}) custom-call(s32[2]{0:T(128)S(1)} %pad_add_fusion.place, bf16[64,400,128]{2,1,0:T(8,128)(2,1)} %all-to-all-done.arrived.whole_arrived, ...), custom_call_target="tpu_custom_call" | custom-call | flops 3276800 | bytes 6553600 | tf_op jit(solution)/shard_map/pallas_call | solution.py:385
  111.5 0.0 collective-permute-done.1
  111.6 0.1 stack.27
  111.6 0.1 stack.28
  111.7 0.1 stack.29
  111.8 0.1 stack.30
  111.9 3.0 %collective-permute-start.7 = (s16[528,256]{1,0:T(8,128)(2,1)S(1)}, s16[528,256]{1,0:T(8,128)(2,1)S(1)}, u32[]{:S(2)}, u32[]{:S(2)}) collective-permute-start(s16[528,256]{1,0:T(8,128)(2,1)S(1)} %get-tuple-element.64), channel_id=1, source_target_pairs={{0,64},{64,128},{128,192},{192,0},{1,65},{65,129},{129,193},{193,1... | collective-permute-start | bytes 811016 | tf_op jit(solution)/shard_map/ppermute | solution.py:768
  114.9 2.0 collective-permute-start.9
  116.9 1.9 collective-permute-start.5
  118.8 0.0 copy-start.2
  118.8 5.3 %shard_map.58 = (bf16[4,256,512]{2,1,0:T(8,128)(2,1)S(1)}, bf16[4,512,256]{2,1,0:T(8,128)(2,1)S(1)}, bf16[4,384,384]{2,1,0:T(8,128)(2,1)S(1)}, bf16[4,384,384]{2...) custom-call(f32[4,93]{1,0:T(4,128)S(1)} %pad_maximum_fusion.taps), custom_call_target="tpu_custom_call" | custom-call | flops 4000000000 | bytes 20000000 | tf_op jit(solution)/shard_map/pallas_call | solution.py:453
  124.0 0.0 collective-permute-done.3.from_left.e_left
  124.0 2.5 %collective-permute-start.6 = (s16[1056,256]{1,0:T(8,128)(2,1)S(1)}, s16[1056,256]{1,0:T(8,128)(2,1)S(1)}, u32[]{:S(2)}, u32[]{:S(2)}) collective-permute-start(s16[1056,256]{1,0:T(8,128)(2,1)S(1)} %get-tuple-element.63), channel_id=1, source_target_pairs={{0,192},{64,0},{128,64},{192,128},{1,193},{65,1},{129,65},{193,129... | collective-permute-start | bytes 1622024 | tf_op jit(solution)/shard_map/ppermute | solution.py:768
  126.6 0.0 collective-permute-done.4.from_right.e_right
  126.6 5.5 %shard_map.59.rest_1_.rest_3_ = f32[4,768,384]{2,1,0:T(8,128)S(1)} custom-call(f32[3,256,384]{2,1,0:T(8,128)S(1)} %copy-done.2, s16[3,128,384]{2,1,0:T(8,128)(2,1)S(1)} %collective-permute-done.3.from_left.e_left, s16[3,128,384]{2,1,0:T(8,128)(2,1)S(1)} %collective-permute-done.4.from_right.e_right, bf16[4,256,512]{2,1,0:T(8,128)(2,1)S(1)} %get-tuple-element.56.kx.rest_5_, ...), custom_call_target="tpu_custom_call" | custom-call | flops 7000000000 | bytes 16000000 | tf_op jit(solution)/shard_map/pallas_call | solution.py:563
  132.1 2.0 shard_map.60.rest_0_
  134.1 1.3 collective-permute-done.7
  135.5 0.7 collective-permute-start.8
  136.2 0.0 collective-permute-done.9
  136.2 3.4 %collective-permute-start.10 = (s16[528,256]{1,0:T(8,128)(2,1)S(1)}, s16[528,256]{1,0:T(8,128)(2,1)S(1)}, u32[]{:S(2)}, u32[]{:S(2)}) collective-permute-start(s16[528,256]{1,0:T(8,128)(2,1)S(1)} %collective-permute-done.9), channel_id=1, source_target_pairs={{0,192},{64,0},{128,64},{192,128},{1,193},{65,1},{129,65},{193,129... | collective-permute-start | bytes 811016 | tf_op jit(solution)/shard_map/ppermute | solution.py:768
  139.6 7.4 %collective-permute-done.5.rest_1_ = s16[1056,256]{1,0:T(8,128)(2,1)S(1)} collective-permute-done((s16[1056,256]{1,0:T(8,128)(2,1)S(1)}, s16[1056,256]{1,0:T(8,128)(2,1)S(1)}, u32[]{:S(2)}, u32[]{:S(2)}) %collective-permute-start.5) | collective-permute-done | bytes 540704 | tf_op jit(solution)/shard_map/ppermute | solution.py:768
  147.0 0.0 collective-permute-done.6.rest_2_.rest_4_
  147.1 3.4 %shard_map.61.rest_0_ = f32[3,512,384]{2,1,0:T(8,128)S(1)} custom-call(s32[2]{0:T(128)S(1)} %pad_add_fusion.place, f32[3,512,384]{2,1,0:T(8,128)S(1)} %shard_map.60.rest_0_, s16[1056,256]{1,0:T(8,128)(2,1)S(1)} %collective-permute-done.5.rest_1_, s16[1056,256]{1,0:T(8,128)(2,1)S(1)} %collective-permute-done.6.rest_2_.rest_4_, ...), custom_call_target="tpu_custom_call" | custom-call | flops 4000000000 | bytes 16000000 | tf_op jit(solution)/shard_map/pallas_call | solution.py:606
  150.4 2.3 collective-permute-done.8.rest_1_.rest_2_
  152.7 9.5 %collective-permute-done.10.rest_2_.rest_3_ = s16[528,256]{1,0:T(8,128)(2,1)S(1)} collective-permute-done((s16[528,256]{1,0:T(8,128)(2,1)S(1)}, s16[528,256]{1,0:T(8,128)(2,1)S(1)}, u32[]{:S(2)}, u32[]{:S(2)}) %collective-permute-start.10) | collective-permute-done | bytes 270368 | tf_op jit(solution)/shard_map/ppermute | solution.py:768
  162.2 2.7 %shard_map.62 = (f32[3,512,384]{2,1,0:T(8,128)S(1)}, s16[992,256]{1,0:T(8,128)(2,1)S(1)}, s16[992,256]{1,0:T(8,128)(2,1)S(1)}) custom-call(s32[2]{0:T(128)S(1)} %pad_add_fusion.place, f32[3,512,384]{2,1,0:T(8,128)S(1)} %shard_map.61.rest_0_, s16[528,256]{1,0:T(8,128)(2,1)S(1)} %collective-permute-done.8.rest_1_.rest_2_, ...), custom_call_target="tpu_custom_call" | custom-call | flops 2000000000 | bytes 8000000 | tf_op jit(solution)/shard_map/pallas_call | solution.py:606
  164.9 1.9 collective-permute-start.11
  166.8 0.1 collective-permute-start.12
  166.9 12.4 %collective-permute-done.11.x_first = s16[992,256]{1,0:T(8,128)(2,1)S(1)} collective-permute-done((s16[992,256]{1,0:T(8,128)(2,1)S(1)}, s16[992,256]{1,0:T(8,128)(2,1)S(1)}, u32[]{:S(2)}, u32[]{:S(2)}) %collective-permute-start.11) | collective-permute-done | bytes 507936 | tf_op jit(solution)/shard_map/ppermute | solution.py:778
  179.4 0.0 collective-permute-done.12.x_second
  179.4 10.5 %shard_map.63 = (f32[3,256,256]{2,1,0:T(8,128)S(1)}, f32[3,256,256]{2,1,0:T(8,128)S(1)}, s16[400,256]{1,0:T(8,128)(2,1)S(1)}, s16[400,256]{1,0:T(8,128)(2,1)S(1)}) custom-call(s32[2]{0:T(128)S(1)} %pad_add_fusion.place, f32[3,256,384]{2,1,0:T(8,128)S(1)} %copy-done.2, s16[3,128,384]{2,1,0:T(8,128)(2,1)S(1)} %collective-permute-done.3.from_left.e_left, ...), custom_call_target="tpu_custom_call" | custom-call | flops 16000000000 | bytes 40000000 | tf_op jit(solution)/shard_map/pallas_call | solution.py:657
  189.8 1.9 collective-permute-start.13
  191.8 0.1 collective-permute-start.14
  191.9 6.8 %collective-permute-done.13.x_first = s16[400,256]{1,0:T(8,128)(2,1)S(1)} collective-permute-done((s16[400,256]{1,0:T(8,128)(2,1)S(1)}, s16[400,256]{1,0:T(8,128)(2,1)S(1)}, u32[]{:S(2)}, u32[]{:S(2)}) %collective-permute-start.13) | collective-permute-done | bytes 204832 | tf_op jit(solution)/shard_map/ppermute | solution.py:778
  198.6 0.0 collective-permute-done.14.x_second
  198.6 1.0 shard_map.64
  199.6 0.1 collective-permute-start.15
  199.7 2.9 %collective-permute-start.17 = (s16[400,256]{1,0:T(8,128)(2,1)S(1)}, s16[400,256]{1,0:T(8,128)(2,1)S(1)}, u32[]{:S(2)}, u32[]{:S(2)}) collective-permute-start(s16[400,256]{1,0:T(8,128)(2,1)S(1)} %get-tuple-element.74.rest_1_), channel_id=1, source_target_pairs={{0,64},{64,128},{128,192},{192,0},{1,65},{65,129},{129,193},{193,1... | collective-permute-start | bytes 614408 | tf_op jit(solution)/shard_map/ppermute | solution.py:768
  202.6 3.8 %collective-permute-start.19 = (s16[400,256]{1,0:T(8,128)(2,1)S(1)}, s16[400,256]{1,0:T(8,128)(2,1)S(1)}, u32[]{:S(2)}, u32[]{:S(2)}) collective-permute-start(s16[400,256]{1,0:T(8,128)(2,1)S(1)} %get-tuple-element.73.rest_0_), channel_id=1, source_target_pairs={{0,64},{64,128},{128,192},{192,0},{1,65},{65,129},{129,193},{193,1... | collective-permute-start | bytes 614408 | tf_op jit(solution)/shard_map/ppermute | solution.py:768
  206.4 0.4 collective-permute-start.20
  206.8 12.8 %collective-permute-done.15.rest_4_ = s16[400,256]{1,0:T(8,128)(2,1)S(1)} collective-permute-done((s16[400,256]{1,0:T(8,128)(2,1)S(1)}, s16[400,256]{1,0:T(8,128)(2,1)S(1)}, u32[]{:S(2)}, u32[]{:S(2)}) %collective-permute-start.15) | collective-permute-done | bytes 204832 | tf_op jit(solution)/shard_map/ppermute | solution.py:768
  219.6 0.0 collective-permute-start.16
  219.6 2.1 collective-permute-done.17.rest_3_
  221.6 1.5 collective-permute-start.18
  223.1 2.9 %collective-permute-done.19.rest_2_ = s16[400,256]{1,0:T(8,128)(2,1)S(1)} collective-permute-done((s16[400,256]{1,0:T(8,128)(2,1)S(1)}, s16[400,256]{1,0:T(8,128)(2,1)S(1)}, u32[]{:S(2)}, u32[]{:S(2)}) %collective-permute-start.19) | collective-permute-done | bytes 204832 | tf_op jit(solution)/shard_map/ppermute | solution.py:768
  226.0 3.0 %shard_map.65._ = f32[24,32,1024]{2,1,0:T(8,128)} custom-call(s32[2]{0:T(128)S(1)} %pad_add_fusion.place, s16[400,256]{1,0:T(8,128)(2,1)S(1)} %get-tuple-element.73.rest_0_, s16[400,256]{1,0:T(8,128)(2,1)S(1)} %get-tuple-element.74.rest_1_, s16[400,256]{1,0:T(8,128)(2,1)S(1)} %collective-permute-done.19.rest_2_, ...), custom_call_target="tpu_custom_call" | custom-call | flops 3000000 | bytes 6000000 | tf_op jit(solution)/shard_map/pallas_call | solution.py:721
  229.0 0.8 collective-permute-done.16.low
  229.8 1.9 collective-permute-done.18.high
  231.7 1.7 shard_map.66
  (13 shorter events, 0.0 us)
Async XLA Ops:
  5.5 9.3 %copy-start.5 = (f32[1,3,31]{2,0,1:T(1,128)S(1)}, f32[1,3,31]{2,0,1:T(1,128)}, u32[]{:S(2)}) copy-start(f32[1,3,31]{2,0,1:T(1,128)} %param.8) | copy-start | bytes 1120
  5.5 18.8 %copy-start = (f32[24,32,1024]{2,1,0:T(8,128)S(1)}, f32[24,32,1024]{2,1,0:T(8,128)}, u32[]{:S(2)}) copy-start(f32[24,32,1024]{2,1,0:T(8,128)} %start) | copy-start | bytes 9437188
  5.5 97.9 %all-to-all-start = ((bf16[64,400,128]{2,1,0:T(8,128)(2,1)}), bf16[64,400,128]{2,1,0:T(8,128)(2,1)}, u32[]{:S(2)}, u32[]{:S(2)}) async-start(bf16[64,400,128]{2,1,0:T(8,128)(2,1)} %shard_map.55), calls=%async_computation | async-start | bytes 13107200 | tf_op jit(solution)/shard_map/all_to_all | solution.py:781
  15.0 96.5 %collective-permute-start.2 = (f32[3,31]{1,0:T(4,128)S(1)}, f32[3,31]{1,0:T(4,128)S(1)}, u32[]{:S(2)}, u32[]{:S(2)}) collective-permute-start(f32[3,31]{1,0:T(4,128)S(1)} %fusion), channel_id=1, source_target_pairs={{0,192},{64,0},{128,64},{192,128},{1,193},{65,1},{129,65},{193,129... | collective-permute-start | bytes 1124 | tf_op jit(solution)/shard_map/ppermute | solution.py:768
  20.4 91.1 %collective-permute-start.1 = (f32[3,31]{1,0:T(4,128)S(1)}, f32[3,31]{1,0:T(4,128)S(1)}, u32[]{:S(2)}, u32[]{:S(2)}) collective-permute-start(f32[3,31]{1,0:T(4,128)S(1)} %fusion), channel_id=1, source_target_pairs={{0,128},{64,192},{128,0},{192,64},{1,129},{65,193},{129,1},{193,65... | collective-permute-start | bytes 1124 | tf_op jit(solution)/shard_map/ppermute | solution.py:768
  21.9 89.7 %collective-permute-start = (f32[3,31]{1,0:T(4,128)S(1)}, f32[3,31]{1,0:T(4,128)S(1)}, u32[]{:S(2)}, u32[]{:S(2)}) collective-permute-start(f32[3,31]{1,0:T(4,128)S(1)} %fusion), channel_id=1, source_target_pairs={{0,64},{64,128},{128,192},{192,0},{1,65},{65,129},{129,193},{193,1... | collective-permute-start | bytes 1124 | tf_op jit(solution)/shard_map/ppermute | solution.py:768
  26.4 1.0 copy-start.1
  27.4 96.7 %collective-permute-start.3 = (s16[3,128,384]{2,1,0:T(8,128)(2,1)}, s16[3,128,384]{2,1,0:T(8,128)(2,1)S(1)}, u32[]{:S(2)}, u32[]{:S(2)}) collective-permute-start(s16[3,128,384]{2,1,0:T(8,128)(2,1)} %get-tuple-element.49), channel_id=1, source_target_pairs={{0,1},{1,2},{2,3},{3,4},{4,5},{5,6},{6,7},{7,8},{8,9},{9,10},{10,1... | collective-permute-start | bytes 884744 | tf_op jit(solution)/shard_map/ppermute | solution.py:772
  29.3 97.3 %collective-permute-start.4 = (s16[3,128,384]{2,1,0:T(8,128)(2,1)}, s16[3,128,384]{2,1,0:T(8,128)(2,1)S(1)}, u32[]{:S(2)}, u32[]{:S(2)}) collective-permute-start(s16[3,128,384]{2,1,0:T(8,128)(2,1)} %get-tuple-element.50), channel_id=1, source_target_pairs={{1,0},{2,1},{3,2},{4,3},{5,4},{6,5},{7,6},{8,7},{9,8},{10,9},{11,1... | collective-permute-start | bytes 884744 | tf_op jit(solution)/shard_map/ppermute | solution.py:772
  111.9 23.6 %collective-permute-start.7 = (s16[528,256]{1,0:T(8,128)(2,1)S(1)}, s16[528,256]{1,0:T(8,128)(2,1)S(1)}, u32[]{:S(2)}, u32[]{:S(2)}) collective-permute-start(s16[528,256]{1,0:T(8,128)(2,1)S(1)} %get-tuple-element.64), channel_id=1, source_target_pairs={{0,64},{64,128},{128,192},{192,0},{1,65},{65,129},{129,193},{193,1... | collective-permute-start | bytes 811016 | tf_op jit(solution)/shard_map/ppermute | solution.py:768
  114.9 21.3 %collective-permute-start.9 = (s16[528,256]{1,0:T(8,128)(2,1)S(1)}, s16[528,256]{1,0:T(8,128)(2,1)S(1)}, u32[]{:S(2)}, u32[]{:S(2)}) collective-permute-start(s16[528,256]{1,0:T(8,128)(2,1)S(1)} %get-tuple-element.65), channel_id=1, source_target_pairs={{0,192},{64,0},{128,64},{192,128},{1,193},{65,1},{129,65},{193,129... | collective-permute-start | bytes 811016 | tf_op jit(solution)/shard_map/ppermute | solution.py:768
  116.9 30.2 %collective-permute-start.5 = (s16[1056,256]{1,0:T(8,128)(2,1)S(1)}, s16[1056,256]{1,0:T(8,128)(2,1)S(1)}, u32[]{:S(2)}, u32[]{:S(2)}) collective-permute-start(s16[1056,256]{1,0:T(8,128)(2,1)S(1)} %get-tuple-element.62), channel_id=1, source_target_pairs={{0,64},{64,128},{128,192},{192,0},{1,65},{65,129},{129,193},{193,1... | collective-permute-start | bytes 1622024 | tf_op jit(solution)/shard_map/ppermute | solution.py:768
  118.8 7.8 %copy-start.2 = (f32[3,256,384]{2,1,0:T(8,128)S(1)}, f32[3,256,384]{2,1,0:T(8,128)}, u32[]{:S(2)}) copy-start(f32[3,256,384]{2,1,0:T(8,128)} %copy-done.1) | copy-start | bytes 3538948
  124.0 23.0 %collective-permute-start.6 = (s16[1056,256]{1,0:T(8,128)(2,1)S(1)}, s16[1056,256]{1,0:T(8,128)(2,1)S(1)}, u32[]{:S(2)}, u32[]{:S(2)}) collective-permute-start(s16[1056,256]{1,0:T(8,128)(2,1)S(1)} %get-tuple-element.63), channel_id=1, source_target_pairs={{0,192},{64,0},{128,64},{192,128},{1,193},{65,1},{129,65},{193,129... | collective-permute-start | bytes 1622024 | tf_op jit(solution)/shard_map/ppermute | solution.py:768
  126.6 5.5 %copy-start.3 = (s16[3,128,384]{2,1,0:T(8,128)(2,1)}, s16[3,128,384]{2,1,0:T(8,128)(2,1)S(1)}, u32[]{:S(2)}) copy-start(s16[3,128,384]{2,1,0:T(8,128)(2,1)S(1)} %collective-permute-done.4.from_right.e_right) | copy-start | bytes 884740
  135.5 17.2 %collective-permute-start.8 = (s16[528,256]{1,0:T(8,128)(2,1)S(1)}, s16[528,256]{1,0:T(8,128)(2,1)S(1)}, u32[]{:S(2)}, u32[]{:S(2)}) collective-permute-start(s16[528,256]{1,0:T(8,128)(2,1)S(1)} %collective-permute-done.7), channel_id=1, source_target_pairs={{0,64},{64,128},{128,192},{192,0},{1,65},{65,129},{129,193},{193,1... | collective-permute-start | bytes 811016 | tf_op jit(solution)/shard_map/ppermute | solution.py:768
  136.2 26.0 %collective-permute-start.10 = (s16[528,256]{1,0:T(8,128)(2,1)S(1)}, s16[528,256]{1,0:T(8,128)(2,1)S(1)}, u32[]{:S(2)}, u32[]{:S(2)}) collective-permute-start(s16[528,256]{1,0:T(8,128)(2,1)S(1)} %collective-permute-done.9), channel_id=1, source_target_pairs={{0,192},{64,0},{128,64},{192,128},{1,193},{65,1},{129,65},{193,129... | collective-permute-start | bytes 811016 | tf_op jit(solution)/shard_map/ppermute | solution.py:768
  150.4 29.0 %copy-start.4 = (s16[3,128,384]{2,1,0:T(8,128)(2,1)S(1)}, s16[3,128,384]{2,1,0:T(8,128)(2,1)}, u32[]{:S(2)}) copy-start(s16[3,128,384]{2,1,0:T(8,128)(2,1)} %copy-done.3) | copy-start | bytes 884740
  164.9 14.5 %collective-permute-start.11 = (s16[992,256]{1,0:T(8,128)(2,1)S(1)}, s16[992,256]{1,0:T(8,128)(2,1)S(1)}, u32[]{:S(2)}, u32[]{:S(2)}) collective-permute-start(s16[992,256]{1,0:T(8,128)(2,1)S(1)} %get-tuple-element.67), channel_id=1, source_target_pairs={{1,2},{2,1},{3,4},{4,3},{5,6},{6,5},{7,8},{8,7},{9,10},{10,9},{11,... | collective-permute-start | bytes 1523720 | tf_op jit(solution)/shard_map/ppermute | solution.py:778
  166.8 12.5 %collective-permute-start.12 = (s16[992,256]{1,0:T(8,128)(2,1)S(1)}, s16[992,256]{1,0:T(8,128)(2,1)S(1)}, u32[]{:S(2)}, u32[]{:S(2)}) collective-permute-start(s16[992,256]{1,0:T(8,128)(2,1)S(1)} %get-tuple-element.68), channel_id=1, source_target_pairs={{0,1},{1,0},{2,3},{3,2},{4,5},{5,4},{6,7},{7,6},{8,9},{9,8},{10,11... | collective-permute-start | bytes 1523720 | tf_op jit(solution)/shard_map/ppermute | solution.py:778
  189.8 8.8 %collective-permute-start.13 = (s16[400,256]{1,0:T(8,128)(2,1)S(1)}, s16[400,256]{1,0:T(8,128)(2,1)S(1)}, u32[]{:S(2)}, u32[]{:S(2)}) collective-permute-start(s16[400,256]{1,0:T(8,128)(2,1)S(1)} %get-tuple-element.71), channel_id=1, source_target_pairs={{1,2},{2,1},{3,4},{4,3},{5,6},{6,5},{7,8},{8,7},{9,10},{10,9},{11,... | collective-permute-start | bytes 614408 | tf_op jit(solution)/shard_map/ppermute | solution.py:778
  191.8 6.9 %collective-permute-start.14 = (s16[400,256]{1,0:T(8,128)(2,1)S(1)}, s16[400,256]{1,0:T(8,128)(2,1)S(1)}, u32[]{:S(2)}, u32[]{:S(2)}) collective-permute-start(s16[400,256]{1,0:T(8,128)(2,1)S(1)} %get-tuple-element.72), channel_id=1, source_target_pairs={{0,1},{1,0},{2,3},{3,2},{4,5},{5,4},{6,7},{7,6},{8,9},{9,8},{10,11... | collective-permute-start | bytes 614408 | tf_op jit(solution)/shard_map/ppermute | solution.py:778
  199.6 19.9 %collective-permute-start.15 = (s16[400,256]{1,0:T(8,128)(2,1)S(1)}, s16[400,256]{1,0:T(8,128)(2,1)S(1)}, u32[]{:S(2)}, u32[]{:S(2)}) collective-permute-start(s16[400,256]{1,0:T(8,128)(2,1)S(1)} %get-tuple-element.73.rest_0_), channel_id=1, source_target_pairs={{0,192},{64,0},{128,64},{192,128},{1,193},{65,1},{129,65},{193,129... | collective-permute-start | bytes 614408 | tf_op jit(solution)/shard_map/ppermute | solution.py:768
  199.7 21.9 %collective-permute-start.17 = (s16[400,256]{1,0:T(8,128)(2,1)S(1)}, s16[400,256]{1,0:T(8,128)(2,1)S(1)}, u32[]{:S(2)}, u32[]{:S(2)}) collective-permute-start(s16[400,256]{1,0:T(8,128)(2,1)S(1)} %get-tuple-element.74.rest_1_), channel_id=1, source_target_pairs={{0,64},{64,128},{128,192},{192,0},{1,65},{65,129},{129,193},{193,1... | collective-permute-start | bytes 614408 | tf_op jit(solution)/shard_map/ppermute | solution.py:768
  202.6 23.4 %collective-permute-start.19 = (s16[400,256]{1,0:T(8,128)(2,1)S(1)}, s16[400,256]{1,0:T(8,128)(2,1)S(1)}, u32[]{:S(2)}, u32[]{:S(2)}) collective-permute-start(s16[400,256]{1,0:T(8,128)(2,1)S(1)} %get-tuple-element.73.rest_0_), channel_id=1, source_target_pairs={{0,64},{64,128},{128,192},{192,0},{1,65},{65,129},{129,193},{193,1... | collective-permute-start | bytes 614408 | tf_op jit(solution)/shard_map/ppermute | solution.py:768
  206.4 19.6 %collective-permute-start.20 = (s16[400,256]{1,0:T(8,128)(2,1)S(1)}, s16[400,256]{1,0:T(8,128)(2,1)S(1)}, u32[]{:S(2)}, u32[]{:S(2)}) collective-permute-start(s16[400,256]{1,0:T(8,128)(2,1)S(1)} %get-tuple-element.74.rest_1_), channel_id=1, source_target_pairs={{0,192},{64,0},{128,64},{192,128},{1,193},{65,1},{129,65},{193,129... | collective-permute-start | bytes 614408 | tf_op jit(solution)/shard_map/ppermute | solution.py:768
  219.6 10.2 %collective-permute-start.16 = (s16[400,256]{1,0:T(8,128)(2,1)S(1)}, s16[400,256]{1,0:T(8,128)(2,1)S(1)}, u32[]{:S(2)}, u32[]{:S(2)}) collective-permute-start(s16[400,256]{1,0:T(8,128)(2,1)S(1)} %collective-permute-done.15.rest_4_), channel_id=1, source_target_pairs={{0,192},{64,0},{128,64},{192,128},{1,193},{65,1},{129,65},{193,129... | collective-permute-start | bytes 614408 | tf_op jit(solution)/shard_map/ppermute | solution.py:768
  221.6 10.0 %collective-permute-start.18 = (s16[400,256]{1,0:T(8,128)(2,1)S(1)}, s16[400,256]{1,0:T(8,128)(2,1)S(1)}, u32[]{:S(2)}, u32[]{:S(2)}) collective-permute-start(s16[400,256]{1,0:T(8,128)(2,1)S(1)} %collective-permute-done.17.rest_3_), channel_id=1, source_target_pairs={{0,64},{64,128},{128,192},{192,0},{1,65},{65,129},{129,193},{193,1... | collective-permute-start | bytes 614408 | tf_op jit(solution)/shard_map/ppermute | solution.py:768
